TPU v7x, 128 devices: a whole 4x4x4 slice. The times are simulated.
128 devices in a mesh: seq: 16 (over z, x_lo, core), head: 8 (over y, x_hi).
Axes of the slice: x: 4 (x_hi: 2, x_lo: 2; x = x_hi * 2 + x_lo), y: 4, z: 4, core: 2. Of those that a mesh axis runs over, the one named last changes fastest.
Arguments:
- queries: bfloat16 [24576, 2048], P(('seq', 'head')), may hold values from -21 to 21
- keys: bfloat16 [24576, 2048], P(('seq', 'head')), may hold values from -21 to 21
- values: bfloat16 [24576, 2048], P(('seq', 'head')), may hold values from -6 to 6
- out_grad: bfloat16 [24576, 2048], P(('seq', 'head')), may hold values from -6 to 6
- block_list: int32 [64, 7], replicated, may hold values from -1 to 63, as said below
Outputs:
- attention_out: bfloat16 [24576, 2048], P(('seq', 'head'))
- grad_q: bfloat16 [24576, 2048], P(('seq', 'head'))
- grad_k: bfloat16 [24576, 2048], P(('seq', 'head'))
- grad_v: bfloat16 [24576, 2048], P(('seq', 'head'))
Inputs may be any that keep to these rules, and one draw needn't show every extreme that they name: `block_list`: row t lists in ascending order the key tiles read by query tile t, then -1 in the remaining entries, and always lists t. A listed tile of another seq index lies within 2 seq indices of t's; over all query tiles of one seq index, at most 2 distinct tiles of any other seq index are listed, and exactly 2 of each seq index one away.
All inputs are finite; a program needn't handle non-finite values.
Results may differ from a plain program's by a relative error of at most 0.025.
Values may be sent and summed in bfloat16 or wider, within the bound.
A program may use at most 192 MiB of HBM per device.

v0:
```python
import jax
import jax.numpy as jnp
from jax import lax
from jax.sharding import PartitionSpec as P

HD = 128
TILE = 384
TILES_DEV = 4
REACH = 2


masked_score = -1e30


def passed_along(block, axis, distance):
    devices = range(lax.axis_size(axis))
    route = [(i - distance, i) for i in devices if i - distance in devices]
    return lax.ppermute(block, axis, route)


def body(queries, keys, values, out_grad, block_list):
    group = lax.axis_size("seq")
    me = lax.axis_index("seq")
    q_loc, k_loc, v_loc, g_loc = (
        lax.all_to_all(queries, "head", split_axis=1, concat_axis=0, tiled=True),
        lax.all_to_all(keys, "head", split_axis=1, concat_axis=0, tiled=True),
        lax.all_to_all(values, "head", split_axis=1, concat_axis=0, tiled=True),
        lax.all_to_all(out_grad, "head", split_axis=1, concat_axis=0, tiled=True),
    )
    width = q_loc.shape[1]
    heads_here = width // HD
    scale = HD ** (-0.5)
    kv_local = jnp.stack((k_loc, v_loc)).reshape(2, TILES_DEV, TILE, width)
    tile_range = jnp.arange(TILES_DEV, dtype=jnp.int32)
    slot_kv = [kv_local]
    slot_ids = [me * TILES_DEV + tile_range]
    send_picks = []
    offsets = [step for step in range(-REACH, REACH + 1) if step != 0]
    for offset in offsets:
        peer = me + offset
        send_pick = jnp.eye(TILES_DEV, dtype=jnp.int32)
        incoming = passed_along(kv_local, "seq", -offset)
        inside = (peer >= 0) & (peer < group)
        live = (jnp.sum(send_pick, axis=1) > 0) & inside
        tile_ids = jnp.sum(send_pick * (peer * TILES_DEV + tile_range)[None, :], axis=1)
        slot_kv.append(incoming)
        slot_ids.append(jnp.where(live, tile_ids, -5))
        send_picks.append(send_pick)
    kv_all = jnp.concatenate(slot_kv, axis=1)
    ids_all = jnp.concatenate(slot_ids)
    slots_all = kv_all.shape[1]
    keys_all = kv_all[0].reshape(slots_all, TILE, heads_here, HD)
    vals_all = kv_all[1].reshape(slots_all, TILE, heads_here, HD)
    my_rows = lax.dynamic_slice_in_dim(block_list, me * TILES_DEV, TILES_DEV, 0)
    q_tiles = q_loc.reshape(TILES_DEV, TILE, heads_here, HD)
    g_tiles = g_loc.reshape(TILES_DEV, TILE, heads_here, HD)

    def one_tile(carry, item):
        acc_keys, acc_vals = carry
        q_tile, g_tile, row = item
        match = (row[:, None] == ids_all[None, :]) & (row[:, None] >= 0)
        valid = jnp.any(match, axis=1)
        slot_of = jnp.argmax(match, axis=1)
        k_sel = keys_all[slot_of]
        v_sel = vals_all[slot_of]
        scores = (
            jnp.einsum("ihd,mjhd->himj", q_tile, k_sel, preferred_element_type=jnp.float32) * scale
        )
        scores = jnp.where(valid[None, None, :, None], scores, masked_score)
        top = jnp.max(scores, axis=(2, 3), keepdims=True)
        expo = jnp.exp(scores - top)
        prob = expo / jnp.sum(expo, axis=(2, 3), keepdims=True)
        prob_b = prob.astype(jnp.bfloat16)
        out_tile = jnp.einsum(
            "himj,mjhd->ihd", prob_b, v_sel, preferred_element_type=jnp.float32
        ).astype(jnp.bfloat16)
        delta = jnp.sum(g_tile.astype(jnp.float32) * out_tile.astype(jnp.float32), axis=2)
        dprob = jnp.einsum("ihd,mjhd->himj", g_tile, v_sel, preferred_element_type=jnp.float32)
        dscore = (prob * (dprob - delta.T[:, :, None, None])).astype(jnp.bfloat16)
        dq_tile = (
            jnp.einsum("himj,mjhd->ihd", dscore, k_sel, preferred_element_type=jnp.float32) * scale
        ).astype(jnp.bfloat16)
        dk_part = (
            jnp.einsum("himj,ihd->mjhd", dscore, q_tile, preferred_element_type=jnp.float32) * scale
        )
        dv_part = jnp.einsum("himj,ihd->mjhd", prob_b, g_tile, preferred_element_type=jnp.float32)
        keep = valid[:, None, None, None]
        acc_keys = acc_keys.at[slot_of].add(jnp.where(keep, dk_part, 0.0))
        acc_vals = acc_vals.at[slot_of].add(jnp.where(keep, dv_part, 0.0))
        return ((acc_keys, acc_vals), (out_tile, dq_tile))

    blank = jnp.zeros((slots_all, TILE, heads_here, HD), jnp.float32)
    (acc_keys, acc_vals), (out_tiles, dq_tiles) = lax.scan(
        one_tile, (blank, blank), (q_tiles, g_tiles, my_rows)
    )
    acc_keys = acc_keys.reshape(slots_all, TILE, width)
    acc_vals = acc_vals.reshape(slots_all, TILE, width)
    own_keys = acc_keys[:TILES_DEV]
    own_vals = acc_vals[:TILES_DEV]
    start = TILES_DEV
    for offset, send_pick in zip(offsets, send_picks):
        count = send_pick.shape[0]
        partial_value = jnp.stack(
            (acc_keys[start : start + count], acc_vals[start : start + count])
        ).astype(jnp.bfloat16)
        start = start + count
        returned = passed_along(partial_value, "seq", offset)
        contrib = returned.astype(jnp.float32)
        own_keys = own_keys + contrib[0]
        own_vals = own_vals + contrib[1]
    attention_out = out_tiles.reshape(TILES_DEV * TILE, width)
    grad_q = dq_tiles.reshape(TILES_DEV * TILE, width)
    grad_k = own_keys.reshape(TILES_DEV * TILE, width).astype(jnp.bfloat16)
    grad_v = own_vals.reshape(TILES_DEV * TILE, width).astype(jnp.bfloat16)
    return (
        lax.all_to_all(attention_out, "head", split_axis=0, concat_axis=1, tiled=True),
        lax.all_to_all(grad_q, "head", split_axis=0, concat_axis=1, tiled=True),
        lax.all_to_all(grad_k, "head", split_axis=0, concat_axis=1, tiled=True),
        lax.all_to_all(grad_v, "head", split_axis=0, concat_axis=1, tiled=True),
    )


def solution(mesh):
    return jax.shard_map(
        body,
        mesh=mesh,
        in_specs=(
            P(("seq", "head"), None),
            P(("seq", "head"), None),
            P(("seq", "head"), None),
            P(("seq", "head"), None),
            P(),
        ),
        out_specs=(
            P(("seq", "head"), None),
            P(("seq", "head"), None),
            P(("seq", "head"), None),
            P(("seq", "head"), None),
        ),
        check_vma=False,
    )
```

profile of v0, /device:TPU:96, one launch (start us, length us, event | category | flops | bytes accessed | tf_op | source)
XLA Modules:
  0.0 688.3 jit_solution(11160870545796479346)
XLA Ops:
  2.8 6.9 %all-to-all-start.1 = ((bf16[192,8,256]{2,0,1:T(8,128)(2,1)}), bf16[192,8,256]{2,0,1:T(8,128)(2,1)S(1)}, u32[]{:S(2)}, u32[]{:S(2)}) async-start(bf16[192,8,256]{2,0,1:T(8,128)(2,1)} %bitcast.115), calls=%async_computation.1 | async-start | bytes 1572864 | tf_op jit(solution)/shard_map/all_to_all | solution.py:26
  9.8 14.3 %all-to-all-done.1 = bf16[192,8,256]{2,0,1:T(8,128)(2,1)S(1)} async-done(((bf16[192,8,256]{2,0,1:T(8,128)(2,1)}), bf16[192,8,256]{2,0,1:T(8,128)(2,1)S(1)}, u32[]{:S(2)}, u32[]{:S(2)}) %all-to-all-start.1) | async-done | bytes 786464 | tf_op jit(solution)/shard_map/all_to_all | solution.py:26
  24.1 16.8 %all_to_all.134 = bf16[192,8,256]{2,0,1:T(8,128)(2,1)S(1)} all-to-all(bf16[192,8,256]{2,0,1:T(8,128)(2,1)S(1)} %bitcast.175), channel_id=1, replica_groups=mesh['seq'=16,'head'=8] {'head'}, dimensions={1} | all-to-all | bytes 1572864 | tf_op jit(solution)/shard_map/all_to_all | solution.py:27
  46.4 3.5 all-to-all-start
  51.9 4.5 collective-permute-start.2
  61.9 29.5 %all-to-all-done = bf16[192,8,256]{2,0,1:T(8,128)(2,1)S(1)} async-done(((bf16[192,8,256]{2,0,1:T(8,128)(2,1)}), bf16[192,8,256]{2,0,1:T(8,128)(2,1)S(1)}, u32[]{:S(2)}, u32[]{:S(2)}) %all-to-all-start) | async-done | bytes 786464 | tf_op jit(solution)/shard_map/all_to_all | solution.py:25
  91.4 3.5 all-to-all-start.3
  96.7 68.1 %all-to-all-done.3 = bf16[192,8,256]{2,0,1:T(8,128)(2,1)S(1)} async-done(((bf16[192,8,256]{2,0,1:T(8,128)(2,1)}), bf16[192,8,256]{2,0,1:T(8,128)(2,1)S(1)}, u32[]{:S(2)}, u32[]{:S(2)}) %all-to-all-start.3) | async-done | bytes 786464 | tf_op jit(solution)/shard_map/all_to_all | solution.py:28
  175.1 5.6 fusion.26
  180.7 8.3 %reshape_squeeze.6 = bf16[20,384,2,128]{3,2,1,0:T(2,128)(2,1)} reshape(bf16[1,20,384,256]{3,2,1,0:T(8,128)(2,1)} %get-tuple-element.166) | data formatting | bytes 7864320 | tf_op jit(solution)/shard_map/reshape;squeeze | solution.py:52
  189.0 8.3 %reshape_squeeze.7 = bf16[20,384,2,128]{3,2,1,0:T(2,128)(2,1)} reshape(bf16[1,20,384,256]{3,2,1,0:T(8,128)(2,1)} %get-tuple-element.165) | data formatting | bytes 7864320 | tf_op jit(solution)/shard_map/reshape;squeeze | solution.py:53
  197.4 4.0 broadcast_in_dim.63
  201.4 4.1 broadcast_in_dim.63.clone
  205.5 290.5 %while.16 = (s32[]{:T(128)}, f32[20,384,2,128]{3,1,2,0:T(8,128)}, f32[20,384,2,128]{3,1,2,0:T(8,128)}, bf16[4,384,2,128]{3,2,1,0:T(2,128)(2,1)}, bf16[4,384,2,12...) while((s32[]{:T(128)}, f32[20,384,2,128]{3,1,2,0:T(8,128)}, ...), condition=%wide.region_13.14_spmd, body=%wide.region_5.13_spmd.sunk | while | flops 3208053248 | bytes 172648688 | solution.py:93
  220.0 5.4 gather_fusion
  232.2 4.1 fusion.65
  236.4 6.6 gather_fusion.1
  243.0 3.9 copy.293
  248.0 5.4 multiply_reduce_fusion.2
  259.4 5.1 select_bitcast_fusion.4
  266.7 6.7 scatter_fusion
  273.4 6.3 select_bitcast_fusion.5
  281.9 6.5 scatter_fusion.1
  289.2 5.4 gather_fusion
  301.4 4.1 fusion.65
  305.6 6.6 gather_fusion.1
  312.2 3.9 copy.293
  317.2 5.4 multiply_reduce_fusion.2
  328.6 5.1 select_bitcast_fusion.4
  335.9 6.6 scatter_fusion
  342.5 6.3 select_bitcast_fusion.5
  351.0 6.4 scatter_fusion.1
  358.2 5.4 gather_fusion
  370.4 4.1 fusion.65
  374.5 6.6 gather_fusion.1
  381.2 3.9 copy.293
  386.2 5.4 multiply_reduce_fusion.2
  397.5 5.1 select_bitcast_fusion.4
  404.9 6.8 scatter_fusion
  411.6 6.3 select_bitcast_fusion.5
  420.1 6.6 scatter_fusion.1
  427.4 5.4 gather_fusion
  439.7 4.1 fusion.65
  443.8 6.6 gather_fusion.1
  450.4 3.9 copy.293
  455.4 5.4 multiply_reduce_fusion.2
  466.8 5.1 select_bitcast_fusion.4
  474.1 6.8 scatter_fusion
  480.9 6.3 select_bitcast_fusion.5
  489.4 6.6 scatter_fusion.1
  496.0 7.2 %copy.208 = bf16[20,384,2,128]{1,3,2,0:T(8,128)(2,1)} copy(f32[20,384,2,128]{3,1,2,0:T(8,128)} %get-tuple-element.67) | data formatting | bytes 11796480 | tf_op jit(solution)/shard_map/while | solution.py:93
  506.3 7.2 %copy.209 = bf16[20,384,2,128]{1,3,2,0:T(8,128)(2,1)} copy(f32[20,384,2,128]{3,1,2,0:T(8,128)} %get-tuple-element.68) | data formatting | bytes 11796480 | tf_op jit(solution)/shard_map/while | solution.py:93
  528.5 5.1 collective-permute-start.7
  544.0 4.2 all-to-all-start.4
  551.3 5.2 collective-permute-done.4
  562.8 26.2 %collective-permute-done.5 = bf16[2,4,384,256]{2,3,1,0:T(8,128)(2,1)} collective-permute-done((bf16[2,4,384,256]{2,3,1,0:T(8,128)(2,1)}, bf16[2,4,384,256]{2,3,1,0:T(8,128)(2,1)}, u32[]{:S(2)}, u32[]{:S(2)}) %collective-permute-start.5) | collective-permute-done | bytes 1572896 | tf_op jit(solution)/shard_map/ppermute | solution.py:18
  600.2 31.6 %all-to-all-done.4 = bf16[8,192,256]{2,1,0:T(8,128)(2,1)} async-done(((bf16[8,192,256]{2,1,0:T(8,128)(2,1)}), bf16[8,192,256]{2,1,0:T(8,128)(2,1)}, u32[]{:S(2)}, u32[]{:S(2)}) %all-to-all-start.4) | async-done | bytes 786464 | tf_op jit(solution)/shard_map/all_to_all | solution.py:116
  631.9 4.2 all-to-all-start.5
  639.1 4.3 add_convert_fusion
  643.4 4.5 all-to-all-done.5
  647.9 4.4 all-to-all-start.7
  664.0 4.3 add_convert_fusion.1
  668.3 7.2 %all-to-all-start.6 = ((bf16[8,192,256]{2,1,0:T(8,128)(2,1)}), bf16[8,192,256]{2,1,0:T(8,128)(2,1)S(1)}, u32[]{:S(2)}, u32[]{:S(2)}) async-start(bf16[8,192,256]{2,1,0:T(8,128)(2,1)} %add_convert_fusion.1), calls=%async_computation.6 | async-start | bytes 1572864 | tf_op jit(solution)/shard_map/all_to_all | solution.py:118
  681.8 5.3 all-to-all-done.6
  (170 shorter events, 174.0 us)
Async XLA Ops:
  0.6 61.2 %copy-start = (s32[64,7]{0,1:T(8,128)S(1)}, s32[64,7]{0,1:T(8,128)}, u32[]{:S(2)}) copy-start(s32[64,7]{0,1:T(8,128)} %param.11) | copy-start | bytes 5380
  0.6 9.1 %copy-start.11 = (bf16[192,2048]{1,0:T(8,128)(2,1)S(1)}, bf16[192,2048]{1,0:T(8,128)(2,1)}, u32[]{:S(2)}) copy-start(bf16[192,2048]{1,0:T(8,128)(2,1)} %param.9) | copy-start | bytes 2359300
  2.8 21.3 %all-to-all-start.1 = ((bf16[192,8,256]{2,0,1:T(8,128)(2,1)}), bf16[192,8,256]{2,0,1:T(8,128)(2,1)S(1)}, u32[]{:S(2)}, u32[]{:S(2)}) async-start(bf16[192,8,256]{2,0,1:T(8,128)(2,1)} %bitcast.115), calls=%async_computation.1 | async-start | bytes 1572864 | tf_op jit(solution)/shard_map/all_to_all | solution.py:26
  40.9 4.5 copy-start.12
  42.9 123.0 %collective-permute-start = (bf16[2,4,384,256]{3,2,1,0:T(8,128)(2,1)}, bf16[2,4,384,256]{3,2,1,0:T(8,128)(2,1)S(1)}, u32[]{:S(2)}, u32[]{:S(2)}) collective-permute-start(bf16[2,4,384,256]{3,2,1,0:T(8,128)(2,1)} %get-tuple-element.183), channel_id=1, source_target_pairs={{0,16},{8,24},{16,32},{24,40},{32,48},{40,56},{48,64},{56,72},{64,... | collective-permute-start | bytes 4718600 | tf_op jit(solution)/shard_map/ppermute | solution.py:18
  46.4 45.0 %all-to-all-start = ((bf16[192,8,256]{2,0,1:T(8,128)(2,1)}), bf16[192,8,256]{2,0,1:T(8,128)(2,1)S(1)}, u32[]{:S(2)}, u32[]{:S(2)}) async-start(bf16[192,8,256]{2,0,1:T(8,128)(2,1)} %bitcast.116), calls=%async_computation | async-start | bytes 1572864 | tf_op jit(solution)/shard_map/all_to_all | solution.py:25
  49.9 117.2 %collective-permute-start.1 = (bf16[2,4,384,256]{3,2,1,0:T(8,128)(2,1)}, bf16[2,4,384,256]{3,2,1,0:T(8,128)(2,1)}, u32[]{:S(2)}, u32[]{:S(2)}) collective-permute-start(bf16[2,4,384,256]{3,2,1,0:T(8,128)(2,1)} %get-tuple-element.183), channel_id=1, source_target_pairs={{0,8},{8,16},{16,24},{24,32},{32,40},{40,48},{48,56},{56,64},{64,7... | collective-permute-start | bytes 4718600 | tf_op jit(solution)/shard_map/ppermute | solution.py:18
  51.9 117.9 %collective-permute-start.2 = (bf16[2,4,384,256]{3,2,1,0:T(8,128)(2,1)}, bf16[2,4,384,256]{3,2,1,0:T(8,128)(2,1)}, u32[]{:S(2)}, u32[]{:S(2)}) collective-permute-start(bf16[2,4,384,256]{3,2,1,0:T(8,128)(2,1)} %get-tuple-element.183), channel_id=1, source_target_pairs={{8,0},{16,8},{24,16},{32,24},{40,32},{48,40},{56,48},{64,56},{72,6... | collective-permute-start | bytes 4718600 | tf_op jit(solution)/shard_map/ppermute | solution.py:18
  58.5 114.0 %collective-permute-start.3 = (bf16[2,4,384,256]{3,2,1,0:T(8,128)(2,1)}, bf16[2,4,384,256]{3,2,1,0:T(8,128)(2,1)}, u32[]{:S(2)}, u32[]{:S(2)}) collective-permute-start(bf16[2,4,384,256]{3,2,1,0:T(8,128)(2,1)} %get-tuple-element.183), channel_id=1, source_target_pairs={{16,0},{24,8},{32,16},{40,24},{48,32},{56,40},{64,48},{72,56},{80,... | collective-permute-start | bytes 4718600 | tf_op jit(solution)/shard_map/ppermute | solution.py:18
  91.4 73.4 %all-to-all-start.3 = ((bf16[192,8,256]{2,0,1:T(8,128)(2,1)}), bf16[192,8,256]{2,0,1:T(8,128)(2,1)S(1)}, u32[]{:S(2)}, u32[]{:S(2)}) async-start(bf16[192,8,256]{2,0,1:T(8,128)(2,1)} %bitcast.113), calls=%async_computation.3 | async-start | bytes 1572864 | tf_op jit(solution)/shard_map/all_to_all | solution.py:28
  248.0 5.7 copy-start.2
  255.1 2.1 copy-start.3
  317.2 5.7 copy-start.2
  324.3 2.1 copy-start.3
  386.2 5.7 copy-start.2
  393.2 2.1 copy-start.3
  455.4 5.7 copy-start.2
  462.5 2.1 copy-start.3
  513.4 2.3 copy-start.10
  517.0 39.5 %collective-permute-start.4 = (bf16[2,4,384,256]{2,3,1,0:T(8,128)(2,1)}, bf16[2,4,384,256]{2,3,1,0:T(8,128)(2,1)}, u32[]{:S(2)}, u32[]{:S(2)}) collective-permute-start(bf16[2,4,384,256]{2,3,1,0:T(8,128)(2,1)} %pad_maximum_fusion.1), channel_id=1, source_target_pairs={{16,0},{24,8},{32,16},{40,24},{48,32},{56,40},{64,48},{72,56},{80,... | collective-permute-start | bytes 4718600 | tf_op jit(solution)/shard_map/ppermute | solution.py:18
  521.5 67.5 %collective-permute-start.5 = (bf16[2,4,384,256]{2,3,1,0:T(8,128)(2,1)}, bf16[2,4,384,256]{2,3,1,0:T(8,128)(2,1)}, u32[]{:S(2)}, u32[]{:S(2)}) collective-permute-start(bf16[2,4,384,256]{2,3,1,0:T(8,128)(2,1)} %pad_maximum_fusion.2), channel_id=1, source_target_pairs={{8,0},{16,8},{24,16},{32,24},{40,32},{48,40},{56,48},{64,56},{72,6... | collective-permute-start | bytes 4718600 | tf_op jit(solution)/shard_map/ppermute | solution.py:18
  524.8 70.6 %collective-permute-start.6 = (bf16[2,4,384,256]{2,3,1,0:T(8,128)(2,1)}, bf16[2,4,384,256]{2,3,1,0:T(8,128)(2,1)S(1)}, u32[]{:S(2)}, u32[]{:S(2)}) collective-permute-start(bf16[2,4,384,256]{2,3,1,0:T(8,128)(2,1)} %pad_maximum_fusion.3), channel_id=1, source_target_pairs={{0,8},{8,16},{16,24},{24,32},{32,40},{40,48},{48,56},{56,64},{64,7... | collective-permute-start | bytes 4718600 | tf_op jit(solution)/shard_map/ppermute | solution.py:18
  528.5 107.6 %collective-permute-start.7 = (bf16[2,4,384,256]{2,3,1,0:T(8,128)(2,1)}, bf16[2,4,384,256]{2,3,1,0:T(8,128)(2,1)S(1)}, u32[]{:S(2)}, u32[]{:S(2)}) collective-permute-start(bf16[2,4,384,256]{2,3,1,0:T(8,128)(2,1)} %pad_maximum_fusion.4), channel_id=1, source_target_pairs={{0,16},{8,24},{16,32},{24,40},{32,48},{40,56},{48,64},{56,72},{64,... | collective-permute-start | bytes 4718600 | tf_op jit(solution)/shard_map/ppermute | solution.py:18
  544.0 87.9 %all-to-all-start.4 = ((bf16[8,192,256]{2,1,0:T(8,128)(2,1)}), bf16[8,192,256]{2,1,0:T(8,128)(2,1)}, u32[]{:S(2)}, u32[]{:S(2)}) async-start(bf16[8,192,256]{2,1,0:T(8,128)(2,1)} %all_to_all.112), calls=%async_computation.4 | async-start | bytes 1572864 | tf_op jit(solution)/shard_map/all_to_all | solution.py:116
  631.9 16.0 %all-to-all-start.5 = ((bf16[8,192,256]{2,1,0:T(8,128)(2,1)}), bf16[8,192,256]{2,1,0:T(8,128)(2,1)}, u32[]{:S(2)}, u32[]{:S(2)}) async-start(bf16[8,192,256]{2,1,0:T(8,128)(2,1)} %all_to_all.116), calls=%async_computation.5 | async-start | bytes 1572864 | tf_op jit(solution)/shard_map/all_to_all | solution.py:117
  637.5 1.7 copy-start.8
  647.9 20.4 %all-to-all-start.7 = ((bf16[8,192,256]{2,1,0:T(8,128)(2,1)}), bf16[8,192,256]{2,1,0:T(8,128)(2,1)}, u32[]{:S(2)}, u32[]{:S(2)}) async-start(bf16[8,192,256]{2,1,0:T(8,128)(2,1)} %add_convert_fusion), calls=%async_computation.7 | async-start | bytes 1572864 | tf_op jit(solution)/shard_map/all_to_all | solution.py:119
  653.8 3.6 copy-start.4
  657.5 1.6 copy-start.5
  659.1 1.7 copy-start.6
  660.7 1.6 copy-start.7
  662.4 1.6 copy-start.9
  668.3 18.8 %all-to-all-start.6 = ((bf16[8,192,256]{2,1,0:T(8,128)(2,1)}), bf16[8,192,256]{2,1,0:T(8,128)(2,1)S(1)}, u32[]{:S(2)}, u32[]{:S(2)}) async-start(bf16[8,192,256]{2,1,0:T(8,128)(2,1)} %add_convert_fusion.1), calls=%async_computation.6 | async-start | bytes 1572864 | tf_op jit(solution)/shard_map/all_to_all | solution.py:118
  675.5 12.6 %copy-start.1 = (s32[64,7]{0,1:T(8,128)S(1)}, s32[64,7]{0,1:T(8,128)}, u32[]{:S(2)}) copy-start(s32[64,7]{0,1:T(8,128)} %param.11) | copy-start | bytes 5380
where the time goes:
time: 696 us; the launch traced here: 688 us
  local copies, waits for them, and re-layouts  232 us (33%)
  waiting for transfers between devices  185 us (27%)
  other arithmetic  96.4 us (14%)
  matrix products  84.3 us (12%)
  starting transfers between devices  58.9 us (8%)
  blocking collectives  16.8 us (2%)
  loops' own time  14.2 us (2%)
    all_to_all x1, waiting for transfers between devices, body(): lax.all_to_all(out_grad, 'head', split_axis=1, concat_axis=0, tiled=True)  68.1 us
    gather x8, local copies, waits for them, and re-layouts, one_tile(): v_sel = vals_all[slot_of]  42.2 us
    all_to_all x1, waiting for transfers between devices, body(): lax.all_to_all(attention_out, 'head', split_axis=0, concat_axis=1, tiled=...  31.6 us
    ppermute x8, waiting for transfers between devices, passed_along(): return lax.ppermute(block, axis, route)  31.5 us
    all_to_all x1, waiting for transfers between devices, body(): lax.all_to_all(queries, 'head', split_axis=1, concat_axis=0, tiled=True)  29.5 us
    gather x8, local copies, waits for them, and re-layouts, one_tile(): k_sel = keys_all[slot_of]  28.9 us
    scatter-add x4, other arithmetic, one_tile(): acc_keys = acc_keys.at[slot_of].add(jnp.where(keep, dk_part, 0.0))  26.8 us
    scatter-add x4, other arithmetic, one_tile(): acc_vals = acc_vals.at[slot_of].add(jnp.where(keep, dv_part, 0.0))  26.1 us
  transfers between devices with their start and end apart: 15, of which 8 were waited for; matrix products, arithmetic and copies ran while one was open for 10% of the time, Pallas kernels for 0%

commit v1 on v0

v1 whole, which is shorter than its diff:
```python
import functools

import jax
import jax.numpy as jnp
from jax import lax
from jax.experimental import pallas as pl
from jax.experimental.pallas import tpu as pltpu
from jax.sharding import PartitionSpec as P

HD = 128
HEADS = 16
TILE = 384
HALF = TILE // 2
TILES_DEV = 4
MAXK = 7
GROUPS = 16
PAIRS = GROUPS // 2
OWN = 2 * TILES_DEV
SIDE = 6
SLOTS = OWN + 2 * SIDE
SCALE = HD**-0.5
LOG2E = 1.4426950408889634
MESH = pl.DeviceIdType.MESH
VMEM_LIMIT = 56 * 2**20


def place():
    seq, head = lax.axis_index("seq"), lax.axis_index("head")
    z, x_lo, core = seq // 4, (seq // 2) % 2, seq % 2
    y, x_hi = head // 2, head % 2
    return z, y, x_hi, x_lo, core


def device(z, y, x_hi, x_lo, core):
    return (z * 4 + x_lo * 2 + core, y * 2 + x_hi)


def chain_neighbour(step):
    z, y, x_hi, x_lo, core = place()
    pair = (2 * z + core + step + PAIRS) % PAIRS
    return device(pair // 2, y, x_hi, x_lo, pair % 2)


def head_devices():
    z, y, x_hi, x_lo, core = place()
    found = []
    for dy in range(4):
        for dx in range(4):
            to_y, to_x = (y + dy) % 4, (2 * x_hi + x_lo + dx) % 4
            found.append((device(z, to_y, to_x // 2, to_x % 2, x_lo), to_y * 4 + to_x))
    return found


def token_devices():
    z, y, x_hi, x_lo, core = place()
    found = []
    for dy in range(4):
        for dx in range(2):
            for dc in range(2):
                at_y, at_x, at_core = (y + dy) % 4, (x_hi + dx) % 2, (core + dc) % 2
                found.append((device(z, at_y, at_x, core, at_core), at_core * 4 + at_y, at_x))
    return found


def greet(devices, is_self):
    barrier = pltpu.get_barrier_semaphore()
    for i, there in enumerate(devices):
        if i == 0:
            @pl.when(jnp.logical_not(is_self))
            def _():
                pl.semaphore_signal(barrier, inc=1, device_id=there, device_id_type=MESH)
        else:
            pl.semaphore_signal(barrier, inc=1, device_id=there, device_id_type=MESH)
    pl.semaphore_wait(barrier, len(devices) - is_self.astype(jnp.int32))


def listed(rows, seq, tile0):
    def one_row(r, found):
        low, high = found
        for m in range(MAXK):
            at = rows[seq * TILES_DEV + r, m] - tile0
            inside = (at >= 0) & (at < TILES_DEV)
            low = jnp.minimum(low, jnp.where(inside, at, TILES_DEV))
            high = jnp.maximum(high, jnp.where(inside, at, -1))
        return low, high

    return lax.fori_loop(0, TILES_DEV, one_row, (jnp.int32(TILES_DEV), jnp.int32(-1)))


def asked(pair, side):
    first = 2 * pair
    if side == 0:
        a, b = (first - 2 + GROUPS) % GROUPS, (first - 1 + GROUPS) % GROUPS
        return ((a, 0), (b, 0), (b, 1))
    e, f = (first + 2) % GROUPS, (first + 3) % GROUPS
    return ((e, 0), (e, 1), (f, 1))


def bring_kernel(rows, q_in, k_in, v_in, g_in, q_out, k_out, v_out, g_out, k_side, v_side, picked, here_sem, send_sem, recv_sem, side_send, side_recv):
    z, y, x_hi, x_lo, core = place()
    pair = 2 * z + core
    is_self = x_lo == core
    left, right = chain_neighbour(-1), chain_neighbour(1)
    greet([d for d, _, _ in token_devices()] + [left, right], is_self)
    arrays = ((k_in, k_out), (v_in, v_out), (q_in, q_out), (g_in, g_out))
    tile, row = core * 4 + y, x_hi * HALF
    targets = head_devices()

    def block(src, dst, head):
        return (
            src.at[:, pl.ds(pl.multiple_of(head * HD, HD), HD)],
            dst.at[tile, pl.ds(pl.multiple_of(row, HALF), HALF)],
        )

    for n, (src, dst) in enumerate(arrays):
        for i, (there, head) in enumerate(targets):
            piece, landing = block(src, dst, head)
            if i == 0:
                @pl.when(is_self)
                def _():
                    pltpu.make_async_copy(piece, landing, recv_sem.at[n]).start()

                @pl.when(jnp.logical_not(is_self))
                def _():
                    pltpu.make_async_remote_copy(piece, landing, here_sem.at[n], recv_sem.at[n], there, MESH).start()
            else:
                pltpu.make_async_remote_copy(piece, landing, send_sem.at[n], recv_sem.at[n], there, MESH).start()

    picks = []
    for side in range(2):
        for seq, which in asked(pair, side):
            low, high = listed(rows, seq, (2 * pair + which) * TILES_DEV)
            picks.append((side, which * TILES_DEV + jnp.minimum(low, TILES_DEV - 1)))
            picks.append((side, which * TILES_DEV + jnp.maximum(high, 0)))

    side_copies = []
    for n, dst, beside in ((0, k_out, k_side), (1, v_out, v_side)):
        pltpu.make_async_copy(dst, dst, recv_sem.at[n]).wait()
        for i, (side, tile_at) in enumerate(picks):
            picked[side, n, i % SIDE] = dst[tile_at]
        for side, there in ((0, left), (1, right)):
            copy = pltpu.make_async_remote_copy(
                picked.at[side, n],
                beside.at[pl.ds((1 - side) * SIDE, SIDE)],
                side_send.at[side, n],
                side_recv.at[side, n],
                there,
                MESH,
            )
            copy.start()
            side_copies.append(copy)
    for n, dst in ((2, q_out), (3, g_out)):
        pltpu.make_async_copy(dst, dst, recv_sem.at[n]).wait()
    for copy in side_copies:
        copy.wait()
    for n, (src, dst) in enumerate(arrays):
        most = src.at[:, pl.ds(0, (HEADS - 1) * HD)]
        pltpu.make_async_copy(most, most, send_sem.at[n]).wait()

        @pl.when(jnp.logical_not(is_self))
        def _():
            one = src.at[:, pl.ds(0, HD)]
            pltpu.make_async_copy(one, one, here_sem.at[n]).wait()


def dot(a, b, over_a, over_b):
    return lax.dot_general(a, b, (((over_a,), (over_b,)), ((), ())), preferred_element_type=jnp.float32)


def lanes(x, op):
    return functools.reduce(op, [x[:, i * HD : (i + 1) * HD] for i in range(x.shape[1] // HD)])


def attend_kernel(rows, q_ref, k_own, v_own, g_ref, k_beside, v_beside, o_ref, dq_ref, dk_own, dv_own, dk_side, dv_side, k_ref, v_ref, slot_of, count_of, score, expo, dk_acc, dv_acc, load_sem):
    loads = []
    for n, (own, beside, whole) in enumerate(((k_own, k_beside, k_ref), (v_own, v_beside, v_ref))):
        loads.append(pltpu.make_async_copy(own, whole.at[pl.ds(0, OWN)], load_sem.at[n, 0]))
        loads.append(pltpu.make_async_copy(beside, whole.at[pl.ds(OWN, 2 * SIDE)], load_sem.at[n, 1]))
    for load in loads:
        load.start()
    z, y, x_hi, x_lo, core = place()
    pair = 2 * z + core
    first_tile = 2 * pair * TILES_DEV
    lows = []
    for which, step in ((0, -2), (0, -1), (1, -2), (0, 2), (1, 1), (1, 2)):
        seq = 2 * pair + which
        lows.append(listed(rows, seq, (seq + step) * TILES_DEV)[0])

    def find(t, _):
        which = t // TILES_DEV

        def entry(m, count):
            at = rows[first_tile + t, m] - first_tile
            step = (at + 2 * TILES_DEV) // TILES_DEV - 2
            inner = at - step * TILES_DEV
            own = (step == 0) | (step == 1)
            side_slot = jnp.where(
                step == -2, 0 + (inner != lows[0]).astype(jnp.int32),
                jnp.where(
                    step == -1,
                    jnp.where(which == 0, 2 + (inner != lows[1]).astype(jnp.int32), 4 + (inner != lows[2]).astype(jnp.int32)),
                    jnp.where(
                        step == 2,
                        jnp.where(which == 0, 6 + (inner != lows[3]).astype(jnp.int32), 8 + (inner != lows[4]).astype(jnp.int32)),
                        10 + (inner != lows[5]).astype(jnp.int32),
                    ),
                ),
            )
            slot_of[t, m] = jnp.where(own, at, OWN + side_slot)
            return count + (rows[first_tile + t, m] >= 0).astype(jnp.int32)

        count_of[t] = lax.fori_loop(0, MAXK, entry, jnp.int32(0))
        return 0

    lax.fori_loop(0, OWN, find, 0)
    dk_acc[...] = jnp.zeros_like(dk_acc)
    dv_acc[...] = jnp.zeros_like(dv_acc)
    for load in loads:
        load.wait()

    def one_tile(t, _):
        count = count_of[t]
        q, g = q_ref[t], g_ref[t]

        def scores(m, top):
            s = dot(q, k_ref[slot_of[t, m]], 1, 1)
            score[m] = s
            return jnp.maximum(top, lanes(s, jnp.maximum))

        top = lax.fori_loop(0, count, scores, jnp.full((TILE, HD), -jnp.inf, jnp.float32))
        top = jnp.max(top, axis=1, keepdims=True)

        def weigh(m, carry):
            total, out = carry
            e = jnp.exp2((score[m] - top) * (SCALE * LOG2E))
            eb = e.astype(jnp.bfloat16)
            expo[m] = eb
            return total + lanes(e, jnp.add), out + dot(eb, v_ref[slot_of[t, m]], 1, 0)

        blank = jnp.zeros((TILE, HD), jnp.float32)
        total, out = lax.fori_loop(0, count, weigh, (blank, blank))
        inv = 1.0 / jnp.sum(total, axis=1, keepdims=True)
        ob = (out * inv).astype(jnp.bfloat16)
        o_ref[t] = ob
        gf = g.astype(jnp.float32)
        delta = jnp.sum(gf * ob.astype(jnp.float32), axis=1, keepdims=True)
        gn = (gf * inv).astype(jnp.bfloat16)
        qn = (q.astype(jnp.float32) * inv).astype(jnp.bfloat16)

        def back(m, dq):
            slot = slot_of[t, m]
            eb = expo[m]
            ds = (eb.astype(jnp.float32) * (dot(g, v_ref[slot], 1, 1) - delta)).astype(jnp.bfloat16)
            dk_acc[slot] += dot(ds, qn, 0, 0)
            dv_acc[slot] += dot(eb, gn, 0, 0)
            return dq + dot(ds, k_ref[slot], 1, 0)

        dq = lax.fori_loop(0, count, back, blank)
        dq_ref[t] = (dq * (inv * SCALE)).astype(jnp.bfloat16)
        return 0

    lax.fori_loop(0, OWN, one_tile, 0)
    dk_own[...] = dk_acc[pl.ds(0, OWN)] * SCALE
    dv_own[...] = dv_acc[pl.ds(0, OWN)]
    dk_side[...] = (dk_acc[pl.ds(OWN, 2 * SIDE)] * SCALE).astype(jnp.bfloat16)
    dv_side[...] = dv_acc[pl.ds(OWN, 2 * SIDE)].astype(jnp.bfloat16)


def return_kernel(rows, o_in, dq_in, dk_own, dv_own, dk_side, dv_side, o_out, dq_out, dk_out, dv_out, k_got, v_got, total, send_sem, recv_sem, side_send, side_recv):
    z, y, x_hi, x_lo, core = place()
    pair = 2 * z + core
    is_self = x_lo == core
    left, right = chain_neighbour(-1), chain_neighbour(1)
    greet([d for d, _ in head_devices()] + [left, right], is_self)
    side_copies = []
    for n, src, got in ((0, dk_side, k_got), (1, dv_side, v_got)):
        for side, there in ((0, left), (1, right)):
            copy = pltpu.make_async_remote_copy(
                src.at[pl.ds(side * SIDE, SIDE)],
                got.at[pl.ds((1 - side) * SIDE, SIDE)],
                side_send.at[side, n],
                side_recv.at[side, n],
                there,
                MESH,
            )
            copy.start()
            side_copies.append(copy)
    head = y * 4 + 2 * x_hi + x_lo
    targets = token_devices()

    def send(n, src, dst):
        for i, (there, tile, half) in enumerate(targets):
            piece = src.at[tile, pl.ds(pl.multiple_of(half * HALF, HALF), HALF)]
            landing = dst.at[:, pl.ds(pl.multiple_of(head * HD, HD), HD)]
            if i == 0:
                @pl.when(is_self)
                def _():
                    pltpu.make_async_copy(piece, landing, recv_sem.at[n]).start()

                @pl.when(jnp.logical_not(is_self))
                def _():
                    pltpu.make_async_remote_copy(piece, landing, send_sem.at[n, 0], recv_sem.at[n], there, MESH).start()
            else:
                pltpu.make_async_remote_copy(piece, landing, send_sem.at[n, 1], recv_sem.at[n], there, MESH).start()

    send(0, o_in, o_out)
    send(1, dq_in, dq_out)
    for got in (k_got, v_got):
        got[2 * SIDE] = jnp.zeros((TILE, HD), jnp.bfloat16)
    asks = []
    for side in range(2):
        for i, (seq, which) in enumerate(asked(pair, side)):
            low, high = listed(rows, seq, (2 * pair + which) * TILES_DEV)
            asks.append((which, side * SIDE + 2 * i, low, high))
    for n, own, got, dst in ((0, dk_own, k_got, dk_out), (1, dv_own, v_got, dv_out)):
        for copy in side_copies[2 * n : 2 * n + 2]:
            copy.wait_recv()
        for u in range(OWN):
            value = own[u]
            for which, slot, low, high in asks:
                if which == u // TILES_DEV:
                    inner = u % TILES_DEV
                    at = jnp.where(low == inner, slot, jnp.where(high == inner, slot + 1, 2 * SIDE))
                    value = value + got[at].astype(jnp.float32)
            total[n, u] = value.astype(jnp.bfloat16)
        send(2 + n, total.at[n], dst)
    for copy in side_copies:
        copy.wait_send()
    for n, (src, dst) in enumerate(((o_in, o_out), (dq_in, dq_out), (total.at[0], dk_out), (total.at[1], dv_out))):
        pltpu.make_async_copy(dst, dst, recv_sem.at[n]).wait()
        most = dst.at[:, pl.ds(0, (HEADS - 1) * HD)]
        pltpu.make_async_copy(most, most, send_sem.at[n, 1]).wait()

        @pl.when(jnp.logical_not(is_self))
        def _():
            one = dst.at[:, pl.ds(0, HD)]
            pltpu.make_async_copy(one, one, send_sem.at[n, 0]).wait()


def shape(*dims, dtype=jnp.bfloat16):
    return jax.ShapeDtypeStruct(dims, dtype)


def body(queries, keys, values, out_grad, block_list):
    vmem, hbm = pl.BlockSpec(memory_space=pltpu.VMEM), pl.BlockSpec(memory_space=pl.ANY)
    smem = pl.BlockSpec(memory_space=pltpu.SMEM)
    dma = pltpu.SemaphoreType.DMA
    q, k, v, g, k_side, v_side = pl.pallas_call(
        bring_kernel,
        out_shape=(shape(OWN, TILE, HD),) * 4 + (shape(2 * SIDE, TILE, HD),) * 2,
        in_specs=[smem] + [hbm] * 4,
        out_specs=(hbm, vmem, vmem, hbm, hbm, hbm),
        scratch_shapes=[
            pltpu.VMEM((2, 2, SIDE, TILE, HD), jnp.bfloat16),
            dma((4,)), dma((4,)), dma((4,)), dma((2, 2)), dma((2, 2)),
        ],
        compiler_params=pltpu.CompilerParams(collective_id=0, has_side_effects=True, vmem_limit_bytes=VMEM_LIMIT),
    )(block_list, queries, keys, values, out_grad)
    f32 = jnp.float32
    o, dq, dk_own, dv_own, dk_side, dv_side = pl.pallas_call(
        attend_kernel,
        out_shape=(
            shape(OWN, TILE, HD), shape(OWN, TILE, HD),
            shape(OWN, TILE, HD, dtype=f32), shape(OWN, TILE, HD, dtype=f32),
            shape(2 * SIDE, TILE, HD), shape(2 * SIDE, TILE, HD),
        ),
        in_specs=[smem, vmem, hbm, hbm, vmem, hbm, hbm],
        out_specs=(vmem,) * 6,
        scratch_shapes=[
            pltpu.VMEM((SLOTS, TILE, HD), jnp.bfloat16),
            pltpu.VMEM((SLOTS, TILE, HD), jnp.bfloat16),
            pltpu.SMEM((OWN, MAXK), jnp.int32),
            pltpu.SMEM((OWN,), jnp.int32),
            pltpu.VMEM((MAXK, TILE, TILE), f32),
            pltpu.VMEM((MAXK, TILE, TILE), jnp.bfloat16),
            pltpu.VMEM((SLOTS, TILE, HD), f32),
            pltpu.VMEM((SLOTS, TILE, HD), f32),
            dma((2, 2)),
        ],
        compiler_params=pltpu.CompilerParams(vmem_limit_bytes=VMEM_LIMIT),
    )(block_list, q, k, v, g, k_side, v_side)
    return pl.pallas_call(
        return_kernel,
        out_shape=(shape(HALF, HEADS * HD),) * 4,
        in_specs=[smem, hbm, hbm, vmem, vmem, hbm, hbm],
        out_specs=(hbm,) * 4,
        scratch_shapes=[
            pltpu.VMEM((2 * SIDE + 1, TILE, HD), jnp.bfloat16),
            pltpu.VMEM((2 * SIDE + 1, TILE, HD), jnp.bfloat16),
            pltpu.VMEM((2, OWN, TILE, HD), jnp.bfloat16),
            dma((4, 2)), dma((4,)), dma((2, 2)), dma((2, 2)),
        ],
        compiler_params=pltpu.CompilerParams(collective_id=1, has_side_effects=True, vmem_limit_bytes=VMEM_LIMIT),
    )(block_list, o, dq, dk_own, dv_own, dk_side, dv_side)


def solution(mesh):
    tokens = P(("seq", "head"), None)
    return jax.shard_map(
        body,
        mesh=mesh,
        in_specs=(tokens, tokens, tokens, tokens, P()),
        out_specs=(tokens, tokens, tokens, tokens),
        check_vma=False,
    )
```

time: 696 us -> 159 us (0.23)
  the two profiles are of different devices: /device:TPU:96 before, /device:TPU:1 now
where the time goes in v1:
time: 159 us; the launch traced here: 157 us
  Pallas kernels  149 us (94%)
  local copies, waits for them, and re-layouts  7.27 us (5%)
    pallas_call x1, Pallas kernels, body(): pl.pallas_call(attend_kernel, out_shape=(shape(OWN, TILE, HD), shape(OWN,...  59.6 us
    pallas_call x1, Pallas kernels, body(): pl.pallas_call(bring_kernel, out_shape=(shape(OWN, TILE, HD),) * 4 + (sha...  45.5 us
    pallas_call x1, Pallas kernels, body(): pl.pallas_call(return_kernel, out_shape=(shape(HALF, HEADS * HD),) * 4, i...  43.9 us
    unnamed x11, local copies, waits for them, and re-layouts  7.27 us

profile of v1, /device:TPU:1, one launch (start us, length us, event | category | flops | bytes accessed | tf_op | source)
XLA Modules:
  0.0 157.0 jit_solution(15494748958746245319)
XLA Ops:
  0.6 1.4 copy.11.rows
  2.0 45.5 %shard_map.84 = (bf16[8,384,128]{2,1,0:T(8,128)(2,1)}, bf16[8,384,128]{2,1,0:T(8,128)(2,1)}, bf16[8,384,128]{2,1,0:T(8,128)(2,1)}, bf16[8,384,128]{2,1,0:T(8,128...) custom-call(s32[64,7]{1,0:T(8,128)} %copy.11.rows, bf16[192,2048]{1,0:T(8,128)(2,1)} %q_in.1, ...), custom_call_target="tpu_custom_call" | custom-call | tf_op jit(solution)/shard_map/pallas_call | solution.py:348
  47.6 59.6 %shard_map.85 = (bf16[8,384,128]{2,1,0:T(8,128)(2,1)}, bf16[8,384,128]{2,1,0:T(8,128)(2,1)}, f32[8,384,128]{2,1,0:T(8,128)}, f32[8,384,128]{2,1,0:T(8,128)}, bf1...) custom-call(s32[64,7]{1,0:T(8,128)} %copy.11.rows, bf16[8,384,128]{2,1,0:T(8,128)(2,1)} %get-tuple-element.16.q_ref, ...), custom_call_target="tpu_custom_call" | custom-call | tf_op jit(solution)/shard_map/pallas_call | solution.py:360
  107.1 43.9 %shard_map.86 = (bf16[192,2048]{1,0:T(8,128)(2,1)}, bf16[192,2048]{1,0:T(8,128)(2,1)}, bf16[192,2048]{1,0:T(8,128)(2,1)}, bf16[192,2048]{1,0:T(8,128)(2,1)}) custom-call(s32[64,7]{1,0:T(8,128)} %copy.11.rows, bf16[8,384,128]{2,1,0:T(8,128)(2,1)} %get-tuple-element.22.o_in, bf16[8,384,128]{2,1,0:T(8,128)(2,1)} %get-tuple-element.23.dq_in, ...), custom_call_target="tpu_custom_call" | custom-call | tf_op jit(solution)/shard_map/pallas_call | solution.py:382
  151.1 0.0 copy-start.2
  151.1 2.2 %copy.16 = bf16[192,2048]{1,0:T(8,128)(2,1)} copy(bf16[192,2048]{1,0:T(8,128)(2,1)} %get-tuple-element.32) | data formatting | bytes 1572864
  153.2 0.0 copy-done.2
  153.3 0.0 copy-start.1
  153.3 0.9 copy.17
  154.1 0.5 copy-done.1
  154.7 0.0 copy-start
  154.7 0.9 copy.18
  155.6 0.5 copy-done
  156.1 0.9 copy.19
Async XLA Ops:
  151.1 2.2 %copy-start.2 = (bf16[192,2048]{1,0:T(8,128)(2,1)S(1)}, bf16[192,2048]{1,0:T(8,128)(2,1)}, u32[]{:S(2)}) copy-start(bf16[192,2048]{1,0:T(8,128)(2,1)} %get-tuple-element.33) | copy-start | bytes 2359300
  153.3 1.4 copy-start.1
  154.7 1.4 copy-start

commit v2 on v1

v2 whole, which is shorter than its diff:
```python
import functools

import jax
import jax.numpy as jnp
from jax import lax
from jax.experimental import pallas as pl
from jax.experimental.pallas import tpu as pltpu
from jax.sharding import PartitionSpec as P

HD = 128
HEADS = 16
TILE = 384
HALF = TILE // 2
TILES_DEV = 4
MAXK = 7
GROUPS = 16
PAIRS = GROUPS // 2
OWN = 2 * TILES_DEV
SIDE = 6
SLOTS = OWN + 2 * SIDE
SCALE = HD**-0.5
LOG2E = 1.4426950408889634
MESH = pl.DeviceIdType.MESH
VMEM_LIMIT = 60 * 2**20


def place():
    seq, head = lax.axis_index("seq"), lax.axis_index("head")
    z, x_lo, core = seq // 4, (seq // 2) % 2, seq % 2
    y, x_hi = head // 2, head % 2
    return z, y, x_hi, x_lo, core


def device(z, y, x_hi, x_lo, core):
    return (z * 4 + x_lo * 2 + core, y * 2 + x_hi)


def chain_neighbour(step):
    z, y, x_hi, x_lo, core = place()
    pair = (2 * z + core + step + PAIRS) % PAIRS
    return device(pair // 2, y, x_hi, x_lo, pair % 2)


def head_devices():
    z, y, x_hi, x_lo, core = place()
    found = []
    for dy in range(4):
        for dx in range(4):
            to_y, to_x = (y + dy) % 4, (2 * x_hi + x_lo + dx) % 4
            found.append((device(z, to_y, to_x // 2, to_x % 2, x_lo), to_y * 4 + to_x))
    return found


def token_devices():
    z, y, x_hi, x_lo, core = place()
    found = []
    for dy in range(4):
        for dx in range(2):
            for dc in range(2):
                at_y, at_x, at_core = (y + dy) % 4, (x_hi + dx) % 2, (core + dc) % 2
                found.append((device(z, at_y, at_x, core, at_core), at_core * 4 + at_y, at_x))
    return found


def greet(devices, is_self):
    barrier = pltpu.get_barrier_semaphore()
    for i, there in enumerate(devices):
        if i == 0:
            @pl.when(jnp.logical_not(is_self))
            def _():
                pl.semaphore_signal(barrier, inc=1, device_id=there, device_id_type=MESH)
        else:
            pl.semaphore_signal(barrier, inc=1, device_id=there, device_id_type=MESH)
    pl.semaphore_wait(barrier, len(devices) - is_self.astype(jnp.int32))


def listed(rows, seq, tile0):
    def one_row(r, found):
        low, high = found
        for m in range(MAXK):
            at = rows[seq * TILES_DEV + r, m] - tile0
            inside = (at >= 0) & (at < TILES_DEV)
            low = jnp.minimum(low, jnp.where(inside, at, TILES_DEV))
            high = jnp.maximum(high, jnp.where(inside, at, -1))
        return low, high

    return lax.fori_loop(0, TILES_DEV, one_row, (jnp.int32(TILES_DEV), jnp.int32(-1)))


def asked(pair, side):
    first = 2 * pair
    if side == 0:
        a, b = (first - 2 + GROUPS) % GROUPS, (first - 1 + GROUPS) % GROUPS
        return ((a, 0), (b, 0), (b, 1))
    e, f = (first + 2) % GROUPS, (first + 3) % GROUPS
    return ((e, 0), (e, 1), (f, 1))


def dot(a, b, over_a, over_b):
    return lax.dot_general(a, b, (((over_a,), (over_b,)), ((), ())), preferred_element_type=jnp.float32)


def eights(x, op):
    return op(x.reshape(x.shape[0] // 8, 8, x.shape[1]), axis=0)


def fill_tables(rows, pair, slot_of, count_of, own_from, side_from):
    first_tile = 2 * pair * TILES_DEV
    lows = []
    for which, step in ((0, -2), (0, -1), (1, -2), (0, 2), (1, 1), (1, 2)):
        seq = 2 * pair + which
        lows.append(listed(rows, seq, (seq + step) * TILES_DEV)[0])

    def later(inner, low):
        return (inner != low).astype(jnp.int32)

    def find(t, _):
        first = t < TILES_DEV
        count = jnp.int32(0)
        for m in range(MAXK):
            entry = rows[first_tile + t, m]
            valid = entry >= 0
            at = jnp.where(valid, entry - first_tile, 0)
            step = (at + 2 * TILES_DEV) // TILES_DEV - 2
            inner = at - step * TILES_DEV
            near_left = jnp.where(first, 2 + later(inner, lows[1]), 4 + later(inner, lows[2]))
            near_right = jnp.where(first, 6 + later(inner, lows[3]), 8 + later(inner, lows[4]))
            beside = jnp.where(
                step == -2,
                later(inner, lows[0]),
                jnp.where(step == -1, near_left, jnp.where(step == 2, near_right, 10 + later(inner, lows[5]))),
            )
            slot_of[t, m] = jnp.where((step == 0) | (step == 1), at, OWN + beside)
            count = count + valid.astype(jnp.int32)
        count_of[t] = count
        return 0

    lax.fori_loop(0, OWN, find, 0)

    def where_listed(t, slot):
        found = jnp.int32(OWN * MAXK)
        count = count_of[t]
        for m in range(MAXK):
            found = jnp.where((slot_of[t, m] == slot) & (count > m), t * MAXK + m, found)
        return found

    def own(u, _):
        def one(t, _):
            own_from[u, t] = where_listed(t, u)
            return 0

        return lax.fori_loop(0, OWN, one, 0)

    lax.fori_loop(0, OWN, own, 0)

    def side(j, _):
        second = ((j >= 4) & (j < 6)) | (j >= 8)
        start = jnp.where(second, TILES_DEV, 0)

        def one(i, _):
            side_from[j, i] = where_listed(start + i, OWN + j)
            return 0

        return lax.fori_loop(0, TILES_DEV, one, 0)

    lax.fori_loop(0, 2 * SIDE, side, 0)


def kernel(
    rows, q_in, k_in, v_in, g_in, o_out, dq_out, dk_out, dv_out,
    q_own, k_own, v_own, g_own, k_side, v_side, picked, k_all, v_all, score, expo, inv_of, delta_of, terms,
    dv_sum, o_done, dq_done, dk_done, dv_done, part, k_got, v_got,
    slot_of, count_of, own_from, side_from,
    in_send, in_recv, out_send, out_recv, side_send, side_recv, back_send, back_recv,
):
    z, y, x_hi, x_lo, core = place()
    pair = 2 * z + core
    is_self = x_lo == core
    left, right = chain_neighbour(-1), chain_neighbour(1)
    greet([d for d, _, _ in token_devices()] + [left, right], is_self)
    arrays = ((k_in, k_own), (v_in, v_own), (q_in, q_own), (g_in, g_own))
    tile, row = core * 4 + y, pl.multiple_of(x_hi * HALF, HALF)
    targets = head_devices()

    for n, (src, dst) in enumerate(arrays):
        for i, (there, head) in enumerate(targets):
            piece = src.at[:, pl.ds(pl.multiple_of(head * HD, HD), HD)]
            landing = dst.at[tile, pl.ds(row, HALF)]
            if i == 0:
                @pl.when(is_self)
                def _():
                    pltpu.make_async_copy(piece, landing, in_recv.at[n]).start()

                @pl.when(jnp.logical_not(is_self))
                def _():
                    pltpu.make_async_remote_copy(piece, landing, in_send.at[n], in_recv.at[n], there, MESH).start()
            else:
                pltpu.make_async_remote_copy(piece, landing, in_send.at[n], in_recv.at[n], there, MESH).start()

    def arrived(n):
        dst = arrays[n][1]
        pltpu.make_async_copy(dst, dst, in_recv.at[n]).wait()

    fill_tables(rows, pair, slot_of, count_of, own_from, side_from)
    asks, picks = [], []
    for side in range(2):
        for i, (seq, which) in enumerate(asked(pair, side)):
            low, high = listed(rows, seq, (2 * pair + which) * TILES_DEV)
            asks.append((which, side * SIDE + 2 * i, low, high))
            picks.append((side, which * TILES_DEV + jnp.minimum(low, TILES_DEV - 1)))
            picks.append((side, which * TILES_DEV + jnp.maximum(high, 0)))
    terms[OWN * MAXK] = jnp.zeros((TILE, HD), jnp.float32)
    for got in (k_got, v_got):
        got[2 * SIDE] = jnp.zeros((TILE, HD), jnp.bfloat16)

    side_copies = []
    for n, own, beside, whole in ((0, k_own, k_side, k_all), (1, v_own, v_side, v_all)):
        arrived(n)
        for i, (side, tile_at) in enumerate(picks):
            picked[side, n, i % SIDE] = own[tile_at]
        for side, there in ((0, left), (1, right)):
            copy = pltpu.make_async_remote_copy(
                picked.at[side, n],
                beside.at[pl.ds((1 - side) * SIDE, SIDE)],
                side_send.at[side, n],
                side_recv.at[side, n],
                there,
                MESH,
            )
            copy.start()
            side_copies.append(copy)
        for u in range(OWN):
            whole[u] = own[u]

    def beside_arrived(n, beside, whole):
        for copy in side_copies[2 * n : 2 * n + 2]:
            copy.wait_recv()
        for j in range(2 * SIDE):
            whole[OWN + j] = beside[j]

    def tile_at(step):
        return ((core + step // TILES_DEV) % 2) * TILES_DEV + (y + step) % TILES_DEV

    head = y * 4 + 2 * x_hi + x_lo

    def send(n, src, dst, t):
        at_y, at_core = t % TILES_DEV, t // TILES_DEV
        for dx in range(2):
            at_x = (x_hi + dx) % 2
            there = device(z, at_y, at_x, core, at_core)
            piece = src.at[t, pl.ds(pl.multiple_of(at_x * HALF, HALF), HALF)]
            landing = dst.at[:, pl.ds(pl.multiple_of(head * HD, HD), HD)]
            remote = pltpu.make_async_remote_copy(piece, landing, out_send.at[n], out_recv.at[n], there, MESH)
            if dx == 0:
                here = is_self & (at_y == y) & (at_core == core)

                @pl.when(here)
                def _():
                    pltpu.make_async_copy(piece, landing, out_recv.at[n]).start()

                @pl.when(jnp.logical_not(here))
                def _():
                    remote.start()
            else:
                remote.start()

    beside_arrived(0, k_side, k_all)
    arrived(2)

    def weigh(step, _):
        t = tile_at(step)
        q, count = q_own[t], count_of[t]
        top = jnp.full((8, TILE), -jnp.inf, jnp.float32)
        for m in range(MAXK):
            s = dot(k_all[slot_of[t, m]], q, 1, 1)
            score[m] = s
            top = jnp.maximum(top, jnp.where(count > m, eights(s, jnp.max), -jnp.inf))
        top = jnp.max(top, axis=0, keepdims=True)
        total = jnp.zeros((8, TILE), jnp.float32)
        for m in range(MAXK):
            e = jnp.exp2((score[m] - jnp.where(count > m, top, 1e30)) * (SCALE * LOG2E))
            expo[t * MAXK + m] = e.astype(jnp.bfloat16)
            total = total + eights(e, jnp.sum)
        inv_of[t] = 1.0 / jnp.sum(total, axis=0, keepdims=True)
        return 0

    lax.fori_loop(0, OWN, weigh, 0)
    beside_arrived(1, v_side, v_all)
    arrived(3)

    def forward(step, _):
        t = tile_at(step)
        inv = inv_of[t]
        g_across = g_own[t].T.astype(jnp.float32)
        g_scaled = (g_across * inv).astype(jnp.bfloat16)
        out = jnp.zeros((HD, TILE), jnp.float32)
        for m in range(MAXK):
            e = expo[t * MAXK + m]
            out = out + dot(v_all[slot_of[t, m]], e, 0, 0)
            terms[t * MAXK + m] = dot(e, g_scaled, 1, 1)
        out = (out * inv).astype(jnp.bfloat16)
        o_done[t] = out.T
        delta_of[t] = jnp.sum(g_across * out.astype(jnp.float32), axis=0, keepdims=True)
        send(0, o_done, o_out, t)
        return 0

    lax.fori_loop(0, OWN, forward, 0)

    back_copies = []

    def send_back(n, got, scale):
        def one(j, _):
            value = terms[side_from[j, 0]]
            for i in range(1, TILES_DEV):
                value = value + terms[side_from[j, i]]
            part[n, j] = (value * scale).astype(jnp.bfloat16)
            return 0

        lax.fori_loop(0, 2 * SIDE, one, 0)
        for side, there in ((0, left), (1, right)):
            copy = pltpu.make_async_remote_copy(
                part.at[n, pl.ds(side * SIDE, SIDE)],
                got.at[pl.ds((1 - side) * SIDE, SIDE)],
                back_send.at[side, n],
                back_recv.at[side, n],
                there,
                MESH,
            )
            copy.start()
            back_copies.append(copy)

    def own_sum(u):
        value = terms[own_from[u, 0]]
        for t in range(1, OWN):
            value = value + terms[own_from[u, t]]
        return value

    def with_got(value, u, got):
        for which, slot, low, high in asks:
            if which == u // TILES_DEV:
                inner = u % TILES_DEV
                value = value + got[jnp.where(low == inner, slot, jnp.where(high == inner, slot + 1, 2 * SIDE))].astype(jnp.float32)
        return value.astype(jnp.bfloat16)

    send_back(0, v_got, 1.0)

    def own_values(u, _):
        dv_sum[u] = own_sum(u)
        return 0

    lax.fori_loop(0, OWN, own_values, 0)

    def backward(step, _):
        t = tile_at(step)
        g, inv, delta = g_own[t], inv_of[t], delta_of[t]
        q_scaled = (q_own[t].T.astype(jnp.float32) * inv).astype(jnp.bfloat16)
        for m in range(MAXK):
            dp = dot(v_all[slot_of[t, m]], g, 1, 1)
            ds = (expo[t * MAXK + m].astype(jnp.float32) * (dp - delta)).astype(jnp.bfloat16)
            expo[t * MAXK + m] = ds
            terms[t * MAXK + m] = dot(ds, q_scaled, 1, 1)
        return 0

    lax.fori_loop(0, 6, backward, 0)
    for copy in back_copies:
        copy.wait_recv()
    for u in range(OWN):
        dv_done[u] = with_got(dv_sum[u], u, v_got)

    def send_values(step, _):
        send(3, dv_done, dv_out, tile_at(step))
        return 0

    lax.fori_loop(0, OWN, send_values, 0)
    lax.fori_loop(6, OWN, backward, 0)
    send_back(1, k_got, SCALE)

    def query_grads(step, _):
        t = tile_at(step)
        dq = jnp.zeros((HD, TILE), jnp.float32)
        for m in range(MAXK):
            dq = dq + dot(k_all[slot_of[t, m]], expo[t * MAXK + m], 0, 0)
        dq_done[t] = (dq * (inv_of[t] * SCALE)).astype(jnp.bfloat16).T
        send(1, dq_done, dq_out, t)
        return 0

    lax.fori_loop(0, OWN, query_grads, 0)
    for copy in back_copies[2:]:
        copy.wait_recv()
    for u in range(OWN):
        dk_done[u] = with_got(own_sum(u) * SCALE, u, k_got)

    def send_keys(step, _):
        send(2, dk_done, dk_out, tile_at(step))
        return 0

    lax.fori_loop(0, OWN, send_keys, 0)

    for copy in side_copies + back_copies:
        copy.wait_send()
    for n, dst in enumerate((o_out, dq_out, dk_out, dv_out)):
        pltpu.make_async_copy(dst, dst, out_recv.at[n]).wait()
        most = dst.at[:, pl.ds(0, (HEADS - 1) * HD)]

        @pl.when(is_self)
        def _():
            pltpu.make_async_copy(most, most, in_send.at[n]).wait()
            pltpu.make_async_copy(most, most, out_send.at[n]).wait()

        @pl.when(jnp.logical_not(is_self))
        def _():
            pltpu.make_async_copy(dst, dst, in_send.at[n]).wait()
            pltpu.make_async_copy(dst, dst, out_send.at[n]).wait()


def body(queries, keys, values, out_grad, block_list):
    hbm, smem = pl.BlockSpec(memory_space=pl.ANY), pl.BlockSpec(memory_space=pltpu.SMEM)
    dma = pltpu.SemaphoreType.DMA

    def tiles(*dims):
        return pltpu.VMEM((*dims, TILE, HD), jnp.bfloat16)

    def counts(*dims):
        return pltpu.SMEM(dims, jnp.int32)

    f32 = jnp.float32
    return pl.pallas_call(
        kernel,
        out_shape=(jax.ShapeDtypeStruct((HALF, HEADS * HD), jnp.bfloat16),) * 4,
        in_specs=[smem] + [hbm] * 4,
        out_specs=(hbm,) * 4,
        scratch_shapes=[
            tiles(OWN), tiles(OWN), tiles(OWN), tiles(OWN),
            tiles(2 * SIDE), tiles(2 * SIDE), tiles(2, 2, SIDE), tiles(SLOTS), tiles(SLOTS),
            pltpu.VMEM((MAXK, TILE, TILE), f32),
            pltpu.VMEM((OWN * MAXK, TILE, TILE), jnp.bfloat16),
            pltpu.VMEM((OWN, 1, TILE), f32),
            pltpu.VMEM((OWN, 1, TILE), f32),
            pltpu.VMEM((OWN * MAXK + 1, TILE, HD), f32),
            pltpu.VMEM((OWN, TILE, HD), f32),
            tiles(OWN), tiles(OWN), tiles(OWN), tiles(OWN),
            tiles(2, 2 * SIDE), tiles(2 * SIDE + 1), tiles(2 * SIDE + 1),
            counts(OWN, MAXK), counts(OWN), counts(OWN, OWN), counts(2 * SIDE, TILES_DEV),
            dma((4,)), dma((4,)), dma((4,)), dma((4,)), dma((2, 2)), dma((2, 2)), dma((2, 2)), dma((2, 2)),
        ],
        compiler_params=pltpu.CompilerParams(collective_id=0, has_side_effects=True, vmem_limit_bytes=VMEM_LIMIT),
    )(block_list, queries, keys, values, out_grad)


def solution(mesh):
    tokens = P(("seq", "head"), None)
    return jax.shard_map(
        body,
        mesh=mesh,
        in_specs=(tokens, tokens, tokens, tokens, P()),
        out_specs=(tokens, tokens, tokens, tokens),
        check_vma=False,
    )
```

time: 159 us -> 110 us (0.69); the launches traced: 157 us -> 110 us
  Pallas kernels: 149 us -> 102 us
    pallas_call x3 -> x1, Pallas kernels: 149 us -> 102 us  [body(): pl.pallas_call(kernel, out_shape=(jax.ShapeDtypeStruct((HALF, HEADS * HD)...]
where the time goes in v2:
time: 110 us
  Pallas kernels  102 us (93%)
  local copies, waits for them, and re-layouts  7.27 us (7%)
    pallas_call x1, Pallas kernels, body(): pl.pallas_call(kernel, out_shape=(jax.ShapeDtypeStruct((HALF, HEADS * HD)...  102 us
    unnamed x11, local copies, waits for them, and re-layouts  7.27 us

profile of v2, /device:TPU:1, one launch (start us, length us, event | category | flops | bytes accessed | tf_op | source)
XLA Modules:
  0.0 109.7 jit_solution(8020049346058459192)
XLA Ops:
  0.6 1.4 %copy.9.rows = s32[64,7]{1,0:T(8,128)} copy(s32[64,7]{0,1:T(8,128)} %param.9) | data formatting | bytes 3584 | tf_op args[4]
  2.0 101.8 %shard_map.84 = (bf16[192,2048]{1,0:T(8,128)(2,1)}, bf16[192,2048]{1,0:T(8,128)(2,1)}, bf16[192,2048]{1,0:T(8,128)(2,1)}, bf16[192,2048]{1,0:T(8,128)(2,1)}) custom-call(s32[64,7]{1,0:T(8,128)} %copy.9.rows, bf16[192,2048]{1,0:T(8,128)(2,1)} %q_in.1, bf16[192,2048]{1,0:T(8,128)(2,1)} %k_in.1, bf16[192,2048]{1,0:T(8,128)(2,1)} %v_in.1, bf16[192,2048]{1,0:T(8,128)(2,1)} %g_in.1), custom_call_target="tpu_custom_call" | custom-call | tf_op jit(solution)/shard_map/pallas_call | solution.py:427
  103.9 0.0 copy-start.2
  103.9 2.2 %copy.14 = bf16[192,2048]{1,0:T(8,128)(2,1)} copy(bf16[192,2048]{1,0:T(8,128)(2,1)} %get-tuple-element.8) | data formatting | bytes 1572864
  106.0 0.0 copy-done.2
  106.0 0.0 copy-start.1
  106.0 0.9 copy.15
  106.9 0.5 copy-done.1
  107.4 0.0 copy-start
  107.4 0.9 copy.16
  108.3 0.5 copy-done
  108.9 0.9 copy.17
Async XLA Ops:
  103.9 2.2 %copy-start.2 = (bf16[192,2048]{1,0:T(8,128)(2,1)S(1)}, bf16[192,2048]{1,0:T(8,128)(2,1)}, u32[]{:S(2)}) copy-start(bf16[192,2048]{1,0:T(8,128)(2,1)} %get-tuple-element.9) | copy-start | bytes 2359300
  106.0 1.4 %copy-start.1 = (bf16[192,2048]{1,0:T(8,128)(2,1)S(1)}, bf16[192,2048]{1,0:T(8,128)(2,1)}, u32[]{:S(2)}) copy-start(bf16[192,2048]{1,0:T(8,128)(2,1)} %get-tuple-element.10) | copy-start | bytes 2359300
  107.4 1.4 %copy-start = (bf16[192,2048]{1,0:T(8,128)(2,1)S(1)}, bf16[192,2048]{1,0:T(8,128)(2,1)}, u32[]{:S(2)}) copy-start(bf16[192,2048]{1,0:T(8,128)(2,1)} %get-tuple-element.11) | copy-start | bytes 2359300

commit v3 on v2

v3 whole, which is shorter than its diff:
```python
import functools

import jax
import jax.numpy as jnp
from jax import lax
from jax.experimental import pallas as pl
from jax.experimental.pallas import tpu as pltpu
from jax.sharding import PartitionSpec as P

HD = 128
HEADS = 16
TILE = 384
HALF = TILE // 2
TILES_DEV = 4
MAXK = 7
GROUPS = 16
PAIRS = GROUPS // 2
OWN = 2 * TILES_DEV
SIDE = 6
SLOTS = OWN + 2 * SIDE
SCALE = HD**-0.5
LOG2E = 1.4426950408889634
MESH = pl.DeviceIdType.MESH
VMEM_LIMIT = 60 * 2**20


def place():
    seq, head = lax.axis_index("seq"), lax.axis_index("head")
    z, x_lo, core = seq // 4, (seq // 2) % 2, seq % 2
    y, x_hi = head // 2, head % 2
    return z, y, x_hi, x_lo, core


def device(z, y, x_hi, x_lo, core):
    return (z * 4 + x_lo * 2 + core, y * 2 + x_hi)


def sides():
    z, y, x_hi, x_lo, core = place()
    toward = 2 * core - 1
    pair = 2 * z + core
    near, far = 2 * pair + core, 2 * pair + 1 - core
    there = device((z + toward + 4) % 4, y, x_hi, x_lo, 1 - core)
    return there, device(z, y, x_hi, x_lo, 1 - core), near, far, toward


def head_devices():
    z, y, x_hi, x_lo, core = place()
    found = []
    for dy in range(4):
        for dx in range(4):
            to_y, to_x = (y + dy) % 4, (2 * x_hi + x_lo + dx) % 4
            found.append((device(z, to_y, to_x // 2, to_x % 2, x_lo), to_y * 4 + to_x))
    return found


def token_devices():
    z, y, x_hi, x_lo, core = place()
    found = []
    for dy in range(4):
        for dx in range(2):
            for dc in range(2):
                at_y, at_x, at_core = (y + dy) % 4, (x_hi + dx) % 2, (core + dc) % 2
                found.append((device(z, at_y, at_x, core, at_core), at_core * 4 + at_y, at_x))
    return found


def greet(devices, is_self):
    barrier = pltpu.get_barrier_semaphore()
    for i, there in enumerate(devices):
        if i == 0:
            @pl.when(jnp.logical_not(is_self))
            def _():
                pl.semaphore_signal(barrier, inc=1, device_id=there, device_id_type=MESH)
        else:
            pl.semaphore_signal(barrier, inc=1, device_id=there, device_id_type=MESH)
    pl.semaphore_wait(barrier, len(devices) - is_self.astype(jnp.int32))


def listed(rows, seq, of):
    row0, tile0 = (seq + GROUPS) % GROUPS * TILES_DEV, of * TILES_DEV

    def one_row(r, found):
        low, high = found
        for m in range(MAXK):
            at = rows[m, row0 + r] - tile0
            inside = (at >= 0) & (at < TILES_DEV)
            low = jnp.minimum(low, jnp.where(inside, at, TILES_DEV))
            high = jnp.maximum(high, jnp.where(inside, at, -1))
        return low, high

    return lax.fori_loop(0, TILES_DEV, one_row, (jnp.int32(TILES_DEV), jnp.int32(-1)))


def asking(near, far, toward):
    mine = (
        (near, near + toward), (near, near + 2 * toward), (far, near + toward),
        (near, far - toward), (far, far - toward), (far, far - 2 * toward),
    )
    theirs = (
        (near + toward, near), (near + toward, far), (near + 2 * toward, near),
        (far - 2 * toward, far), (far - toward, far), (far - toward, near),
    )
    return mine, theirs


def dot(a, b, over_a, over_b):
    return lax.dot_general(a, b, (((over_a,), (over_b,)), ((), ())), preferred_element_type=jnp.float32)


def eights(x, op):
    return op(x.reshape(x.shape[0] // 8, 8, x.shape[1]), axis=0)


def fill_tables(rows, near, far, toward, mine, slot_of, count_of, own_from, side_from):
    first_tile = jnp.minimum(near, far) * TILES_DEV
    near_tile, far_tile = near * TILES_DEV - first_tile, far * TILES_DEV - first_tile
    lows = [listed(rows, seq, of)[0] for seq, of in mine]

    def find(t, _):
        is_near = t // TILES_DEV == near_tile // TILES_DEV
        count = jnp.int32(0)
        for m in range(MAXK):
            entry = rows[m, first_tile + t]
            valid = entry >= 0
            at = jnp.where(valid, entry, first_tile)
            away = (at // TILES_DEV - near) * toward
            inner = at % TILES_DEV
            slots = [2 * i + (inner != low).astype(jnp.int32) for i, low in enumerate(lows)]
            beside = jnp.where(
                away == 1,
                jnp.where(is_near, slots[0], slots[2]),
                jnp.where(away == 2, slots[1], jnp.where(away == -2, jnp.where(is_near, slots[3], slots[4]), slots[5])),
            )
            slot_of[t, m] = jnp.where((away == 0) | (away == -1), at - first_tile, OWN + beside)
            count = count + valid.astype(jnp.int32)
        count_of[t] = count
        return 0

    lax.fori_loop(0, OWN, find, 0)

    def where_listed(t, slot):
        found = jnp.int32(OWN * MAXK)
        count = count_of[t]
        for m in range(MAXK):
            found = jnp.where((slot_of[t, m] == slot) & (count > m), t * MAXK + m, found)
        return found

    def own(u, _):
        def one(t, _):
            own_from[u, t] = where_listed(t, u)
            return 0

        return lax.fori_loop(0, OWN, one, 0)

    lax.fori_loop(0, OWN, own, 0)

    def side(j, _):
        of_far = ((j >= 4) & (j < 6)) | (j >= 8)
        start = jnp.where(of_far, far_tile, near_tile)

        def one(i, _):
            side_from[j, i] = where_listed(start + i, OWN + j)
            return 0

        return lax.fori_loop(0, TILES_DEV, one, 0)

    lax.fori_loop(0, 2 * SIDE, side, 0)


def kernel(
    rows_in, q_in, k_in, v_in, g_in, o_out, dq_out, dk_out, dv_out,
    q_own, k_own, v_own, g_own, k_side, v_side, picked, k_all, v_all, score, expo, inv_of, delta_of, terms,
    dv_sum, o_done, dq_done, dk_done, dv_done, part, k_got, v_got,
    rows, slot_of, count_of, own_from, side_from,
    rows_sem, in_send, in_recv, out_send, out_recv, side_send, side_recv, back_send, back_recv,
):
    z, y, x_hi, x_lo, core = place()
    is_self = x_lo == core
    z_side, core_side, near, far, toward = sides()
    mine, theirs = asking(near, far, toward)
    rows_copy = pltpu.make_async_copy(rows_in, rows, rows_sem)
    rows_copy.start()
    greet([d for d, _, _ in token_devices()] + [z_side, core_side], is_self)
    arrays = ((k_in, k_own), (q_in, q_own), (v_in, v_own), (g_in, g_own))
    tile, row = core * 4 + y, pl.multiple_of(x_hi * HALF, HALF)
    targets = head_devices()

    for n, (src, dst) in enumerate(arrays):
        for i, (there, head) in enumerate(targets):
            piece = src.at[:, pl.ds(pl.multiple_of(head * HD, HD), HD)]
            landing = dst.at[tile, pl.ds(row, HALF)]
            if i == 0:
                @pl.when(is_self)
                def _():
                    pltpu.make_async_copy(piece, landing, in_recv.at[n]).start()

                @pl.when(jnp.logical_not(is_self))
                def _():
                    pltpu.make_async_remote_copy(piece, landing, in_send.at[n], in_recv.at[n], there, MESH).start()
            else:
                pltpu.make_async_remote_copy(piece, landing, in_send.at[n], in_recv.at[n], there, MESH).start()

    def arrived(n):
        dst = arrays[n][1]
        pltpu.make_async_copy(dst, dst, in_recv.at[n]).wait()

    rows_copy.wait()
    fill_tables(rows, near, far, toward, mine, slot_of, count_of, own_from, side_from)
    near_tile, far_tile = core * TILES_DEV, (1 - core) * TILES_DEV
    asks = []
    for i, (seq, of) in enumerate(theirs):
        low, high = listed(rows, seq, of)
        asks.append((i in (0, 2, 5), 2 * i, low, high))
    terms[OWN * MAXK] = jnp.zeros((TILE, HD), jnp.float32)
    for got in (k_got, v_got):
        got[2 * SIDE] = jnp.zeros((TILE, HD), jnp.bfloat16)

    side_copies = []

    def to_sides(n, own, beside, whole):
        for of_near, slot, low, high in asks:
            start = near_tile if of_near else far_tile
            picked[n, slot] = own[start + jnp.minimum(low, TILES_DEV - 1)]
            picked[n, slot + 1] = own[start + jnp.maximum(high, 0)]
        for side, there in ((0, z_side), (1, core_side)):
            span = pl.ds(side * SIDE, SIDE)
            copy = pltpu.make_async_remote_copy(
                picked.at[n, span], beside.at[span], side_send.at[side, n], side_recv.at[side, n], there, MESH
            )
            copy.start()
            side_copies.append(copy)
        for u in range(OWN):
            whole[u] = own[u]

    def beside_arrived(n, beside, whole):
        for copy in side_copies[2 * n : 2 * n + 2]:
            copy.wait_recv()
        for j in range(2 * SIDE):
            whole[OWN + j] = beside[j]

    def tile_at(step):
        return ((core + step // TILES_DEV) % 2) * TILES_DEV + (y + step) % TILES_DEV

    head = y * 4 + 2 * x_hi + x_lo

    def send(n, src, dst, t):
        at_y, at_core = t % TILES_DEV, t // TILES_DEV
        for dx in range(2):
            at_x = (x_hi + dx) % 2
            there = device(z, at_y, at_x, core, at_core)
            piece = src.at[t, pl.ds(pl.multiple_of(at_x * HALF, HALF), HALF)]
            landing = dst.at[:, pl.ds(pl.multiple_of(head * HD, HD), HD)]
            remote = pltpu.make_async_remote_copy(piece, landing, out_send.at[n], out_recv.at[n], there, MESH)
            if dx == 0:
                here = is_self & (at_y == y) & (at_core == core)

                @pl.when(here)
                def _():
                    pltpu.make_async_copy(piece, landing, out_recv.at[n]).start()

                @pl.when(jnp.logical_not(here))
                def _():
                    remote.start()
            else:
                remote.start()

    def each(start, stop, do):
        def one(step, _):
            do(tile_at(step))
            return 0

        lax.fori_loop(start, stop, one, 0)

    def weigh(t):
        q, count = q_own[t], count_of[t]
        top = jnp.full((8, TILE), -jnp.inf, jnp.float32)
        for m in range(MAXK):
            s = dot(k_all[slot_of[t, m]], q, 1, 1)
            score[m] = s
            top = jnp.maximum(top, jnp.where(count > m, eights(s, jnp.max), -jnp.inf))
        top = jnp.max(top, axis=0, keepdims=True)
        total = jnp.zeros((8, TILE), jnp.float32)
        for m in range(MAXK):
            e = jnp.exp2((score[m] - jnp.where(count > m, top, 1e30)) * (SCALE * LOG2E))
            expo[t * MAXK + m] = e.astype(jnp.bfloat16)
            total = total + eights(e, jnp.sum)
        inv_of[t] = 1.0 / jnp.sum(total, axis=0, keepdims=True)

    def value_terms(t):
        g_scaled = (g_own[t].T.astype(jnp.float32) * inv_of[t]).astype(jnp.bfloat16)
        for m in range(MAXK):
            terms[t * MAXK + m] = dot(expo[t * MAXK + m], g_scaled, 1, 1)

    def output(t):
        out = jnp.zeros((HD, TILE), jnp.float32)
        for m in range(MAXK):
            out = out + dot(v_all[slot_of[t, m]], expo[t * MAXK + m], 0, 0)
        out = (out * inv_of[t]).astype(jnp.bfloat16)
        o_done[t] = out.T
        send(0, o_done, o_out, t)
        delta_of[t] = jnp.sum(g_own[t].T.astype(jnp.float32) * out.astype(jnp.float32), axis=0, keepdims=True)

    def backward(t):
        g, delta = g_own[t], delta_of[t]
        q_scaled = (q_own[t].T.astype(jnp.float32) * inv_of[t]).astype(jnp.bfloat16)
        for m in range(MAXK):
            dp = dot(v_all[slot_of[t, m]], g, 1, 1)
            ds = (expo[t * MAXK + m].astype(jnp.float32) * (dp - delta)).astype(jnp.bfloat16)
            expo[t * MAXK + m] = ds
            terms[t * MAXK + m] = dot(ds, q_scaled, 1, 1)

    def query_grad(t):
        dq = jnp.zeros((HD, TILE), jnp.float32)
        for m in range(MAXK):
            dq = dq + dot(k_all[slot_of[t, m]], expo[t * MAXK + m], 0, 0)
        dq_done[t] = (dq * (inv_of[t] * SCALE)).astype(jnp.bfloat16).T
        send(1, dq_done, dq_out, t)

    back_copies = {}

    def send_back(n, half, got, scale):
        def one(j, _):
            value = terms[side_from[j, 0]]
            for i in range(1, TILES_DEV):
                value = value + terms[side_from[j, i]]
            part[n, j] = (value * scale).astype(jnp.bfloat16)
            return 0

        for side, there, first, count in (((0, z_side, 0, 4), (1, core_side, 6, 2)), ((0, z_side, 4, 2), (1, core_side, 8, 4)))[half]:
            lax.fori_loop(first, first + count, one, 0)
            span = pl.ds(first, count)
            copy = pltpu.make_async_remote_copy(
                part.at[n, span], got.at[span], back_send.at[n, half, side], back_recv.at[n, half, side], there, MESH
            )
            copy.start()
            back_copies[n, half, side] = copy

    def own_sum(u):
        value = terms[own_from[u, 0]]
        for t in range(1, OWN):
            value = value + terms[own_from[u, t]]
        return value

    def finish(n, got, own, done):
        for half in range(2):
            for side in range(2):
                back_copies[n, half, side].wait_recv()
        for of_near_tile, start in ((True, near_tile), (False, far_tile)):
            for inner in range(TILES_DEV):
                value = own(start + inner)
                for of_near, slot, low, high in asks:
                    if of_near == of_near_tile:
                        at = jnp.where(low == inner, slot, jnp.where(high == inner, slot + 1, 2 * SIDE))
                        value = value + got[at].astype(jnp.float32)
                done[start + inner] = value.astype(jnp.bfloat16)

    arrived(0)
    to_sides(0, k_own, k_side, k_all)
    beside_arrived(0, k_side, k_all)
    arrived(1)
    each(0, 5, weigh)
    arrived(2)
    to_sides(1, v_own, v_side, v_all)
    each(5, OWN, weigh)
    arrived(3)
    each(0, TILES_DEV, value_terms)
    send_back(0, 0, v_got, 1.0)
    each(TILES_DEV, OWN, value_terms)
    send_back(0, 1, v_got, 1.0)

    def own_values(u, _):
        dv_sum[u] = own_sum(u)
        return 0

    lax.fori_loop(0, OWN, own_values, 0)
    beside_arrived(1, v_side, v_all)
    each(0, OWN, output)
    each(0, 1, backward)
    finish(0, v_got, lambda u: dv_sum[u], dv_done)
    each(0, OWN, lambda t: send(3, dv_done, dv_out, t))
    each(1, TILES_DEV, backward)
    send_back(1, 0, k_got, SCALE)
    each(TILES_DEV, OWN, backward)
    send_back(1, 1, k_got, SCALE)
    each(0, OWN, query_grad)
    finish(1, k_got, lambda u: own_sum(u) * SCALE, dk_done)
    each(0, OWN, lambda t: send(2, dk_done, dk_out, t))

    for copy in side_copies + list(back_copies.values()):
        copy.wait_send()
    for n, dst in enumerate((o_out, dq_out, dk_out, dv_out)):
        pltpu.make_async_copy(dst, dst, out_recv.at[n]).wait()
        most = dst.at[:, pl.ds(0, (HEADS - 1) * HD)]

        @pl.when(is_self)
        def _():
            pltpu.make_async_copy(most, most, in_send.at[n]).wait()
            pltpu.make_async_copy(most, most, out_send.at[n]).wait()

        @pl.when(jnp.logical_not(is_self))
        def _():
            pltpu.make_async_copy(dst, dst, in_send.at[n]).wait()
            pltpu.make_async_copy(dst, dst, out_send.at[n]).wait()


def hand_over(*refs):
    sources, results, (held, in_sem, out_sem) = refs[:4], refs[4:8], refs[8:]
    ins, outs = [], []
    for n in range(4):
        for i in range(2):
            part = pl.ds(i * HALF // 2, HALF // 2)
            ins.append(pltpu.make_async_copy(sources[n].at[part], held.at[n, part], in_sem.at[n, i]))
            outs.append(pltpu.make_async_copy(held.at[n, part], results[n].at[part], out_sem.at[n, i]))
    for copy in ins:
        copy.start()
    for arriving, leaving in zip(ins, outs):
        arriving.wait()
        leaving.start()
    for copy in outs:
        copy.wait()


def body(queries, keys, values, out_grad, block_list):
    hbm = pl.BlockSpec(memory_space=pl.ANY)
    dma = pltpu.SemaphoreType.DMA

    def tiles(*dims):
        return pltpu.VMEM((*dims, TILE, HD), jnp.bfloat16)

    def counts(*dims):
        return pltpu.SMEM(dims, jnp.int32)

    f32 = jnp.float32
    results = (jax.ShapeDtypeStruct((HALF, HEADS * HD), jnp.bfloat16),) * 4
    found = pl.pallas_call(
        kernel,
        out_shape=results,
        in_specs=[hbm] * 5,
        out_specs=(hbm,) * 4,
        scratch_shapes=[
            tiles(OWN), tiles(OWN), tiles(OWN), tiles(OWN),
            tiles(2 * SIDE), tiles(2 * SIDE), tiles(2, 2 * SIDE), tiles(SLOTS), tiles(SLOTS),
            pltpu.VMEM((MAXK, TILE, TILE), f32),
            pltpu.VMEM((OWN * MAXK, TILE, TILE), jnp.bfloat16),
            pltpu.VMEM((OWN, 1, TILE), f32),
            pltpu.VMEM((OWN, 1, TILE), f32),
            pltpu.VMEM((OWN * MAXK + 1, TILE, HD), f32),
            pltpu.VMEM((OWN, TILE, HD), f32),
            tiles(OWN), tiles(OWN), tiles(OWN), tiles(OWN),
            tiles(2, 2 * SIDE), tiles(2 * SIDE + 1), tiles(2 * SIDE + 1),
            counts(MAXK, 4 * GROUPS), counts(OWN, MAXK), counts(OWN), counts(OWN, OWN), counts(2 * SIDE, TILES_DEV),
            pltpu.SemaphoreType.DMA, dma((4,)), dma((4,)), dma((4,)), dma((4,)),
            dma((2, 2)), dma((2, 2)), dma((2, 2, 2)), dma((2, 2, 2)),
        ],
        compiler_params=pltpu.CompilerParams(collective_id=0, has_side_effects=True, vmem_limit_bytes=VMEM_LIMIT),
    )(block_list.T, queries, keys, values, out_grad)
    return pl.pallas_call(
        hand_over,
        out_shape=results,
        in_specs=[hbm] * 4,
        out_specs=(hbm,) * 4,
        scratch_shapes=[pltpu.VMEM((4, HALF, HEADS * HD), jnp.bfloat16), dma((4, 2)), dma((4, 2))],
    )(*found)


def solution(mesh):
    tokens = P(("seq", "head"), None)
    return jax.shard_map(
        body,
        mesh=mesh,
        in_specs=(tokens, tokens, tokens, tokens, P()),
        out_specs=(tokens, tokens, tokens, tokens),
        check_vma=False,
    )
```

time: 110 us -> 100 us (0.909)
  local copies, waits for them, and re-layouts: 7.27 us -> 0 us
  Pallas kernels: 102 us -> 98.3 us
    unnamed x11 -> x0, local copies, waits for them, and re-layouts: 7.27 us -> none
    pallas_call x1 -> x2, Pallas kernels: 102 us -> 98.3 us  [the longest x1 95.5 us: body(): pl.pallas_call(kernel, out_shape=results, in_specs=[hbm] * 5, out_specs=(...]
where the time goes in v3:
time: 100 us; the launch traced here: 98.9 us
  Pallas kernels  98.3 us (98%)
    pallas_call x1, Pallas kernels, body(): pl.pallas_call(kernel, out_shape=results, in_specs=[hbm] * 5, out_specs=(...  95.5 us
    pallas_call x1, Pallas kernels, body(): pl.pallas_call(hand_over, out_shape=results, in_specs=[hbm] * 4, out_spec...  2.79 us

profile of v3, /device:TPU:1, one launch (start us, length us, event | category | flops | bytes accessed | tf_op | source)
XLA Modules:
  0.0 98.9 jit_solution(6952435615221961479)
XLA Ops:
  0.6 95.5 %shard_map.84 = (bf16[192,2048]{1,0:T(8,128)(2,1)}, bf16[192,2048]{1,0:T(8,128)(2,1)}, bf16[192,2048]{1,0:T(8,128)(2,1)}, bf16[192,2048]{1,0:T(8,128)(2,1)}) custom-call(s32[7,64]{1,0:T(8,128)} %bitcast.1, bf16[192,2048]{1,0:T(8,128)(2,1)} %q_in.1, bf16[192,2048]{1,0:T(8,128)(2,1)} %k_in.1, bf16[192,2048]{1,0:T(8,128)(2,1)} %v_in.1, bf16[192,2048]{1,0:T(8,128)(2,1)} %g_in.1), custom_call_target="tpu_custom_call" | custom-call | tf_op jit(solution)/shard_map/pallas_call | solution.py:436
  96.1 2.8 %shard_map.85 = (bf16[192,2048]{1,0:T(8,128)(2,1)}, bf16[192,2048]{1,0:T(8,128)(2,1)}, bf16[192,2048]{1,0:T(8,128)(2,1)}, bf16[192,2048]{1,0:T(8,128)(2,1)}) custom-call(bf16[192,2048]{1,0:T(8,128)(2,1)} %get-tuple-element.8.refs_0_, bf16[192,2048]{1,0:T(8,128)(2,1)} %get-tuple-element.9.refs_1_, bf16[192,2048]{1,0:T(8,128)(2,1)} %get-tuple-element.10.refs_2_, ...), custom_call_target="tpu_custom_call" | custom-call | tf_op jit(solution)/shard_map/pallas_call | solution.py:458

commit v4 on v3

--- a/solution.py
+++ b/solution.py
@@ -240,7 +240,9 @@
             whole[OWN + j] = beside[j]
 
     def tile_at(step):
-        return ((core + step // TILES_DEV) % 2) * TILES_DEV + (y + step) % TILES_DEV
+        turn = step % TILES_DEV
+        away = jnp.where(turn == 0, 2, jnp.where(turn == 3, 0, jnp.where((turn == 1) == (core == 0), 1, 3)))
+        return ((core + step // TILES_DEV) % 2) * TILES_DEV + (y + away) % TILES_DEV
 
     head = y * 4 + 2 * x_hi + x_lo
 
@@ -265,12 +267,13 @@
             else:
                 remote.start()
 
-    def each(start, stop, do):
-        def one(step, _):
-            do(tile_at(step))
+    def each(start, stop, do, by=1):
+        def some(turn, _):
+            for i in range(by):
+                do(tile_at(start + turn * by + i))
             return 0
 
-        lax.fori_loop(start, stop, one, 0)
+        lax.fori_loop(0, (stop - start) // by, some, 0)
 
     def weigh(t):
         q, count = q_own[t], count_of[t]
@@ -287,10 +290,12 @@
             total = total + eights(e, jnp.sum)
         inv_of[t] = 1.0 / jnp.sum(total, axis=0, keepdims=True)
 
+    def row(t):
+        return expo[pl.ds(t * MAXK, MAXK)].reshape(MAXK * TILE, TILE)
+
     def value_terms(t):
         g_scaled = (g_own[t].T.astype(jnp.float32) * inv_of[t]).astype(jnp.bfloat16)
-        for m in range(MAXK):
-            terms[t * MAXK + m] = dot(expo[t * MAXK + m], g_scaled, 1, 1)
+        terms[pl.ds(t * MAXK, MAXK)] = dot(row(t), g_scaled, 1, 1).reshape(MAXK, TILE, HD)
 
     def output(t):
         out = jnp.zeros((HD, TILE), jnp.float32)
@@ -308,7 +313,7 @@
             dp = dot(v_all[slot_of[t, m]], g, 1, 1)
             ds = (expo[t * MAXK + m].astype(jnp.float32) * (dp - delta)).astype(jnp.bfloat16)
             expo[t * MAXK + m] = ds
-            terms[t * MAXK + m] = dot(ds, q_scaled, 1, 1)
+        terms[pl.ds(t * MAXK, MAXK)] = dot(row(t), q_scaled, 1, 1).reshape(MAXK, TILE, HD)
 
     def query_grad(t):
         dq = jnp.zeros((HD, TILE), jnp.float32)
@@ -364,26 +369,26 @@
     to_sides(1, v_own, v_side, v_all)
     each(5, OWN, weigh)
     arrived(3)
-    each(0, TILES_DEV, value_terms)
+    each(0, TILES_DEV, value_terms, 4)
     send_back(0, 0, v_got, 1.0)
-    each(TILES_DEV, OWN, value_terms)
+    each(TILES_DEV, OWN, value_terms, 4)
     send_back(0, 1, v_got, 1.0)
+    beside_arrived(1, v_side, v_all)
+    each(0, OWN, output, 2)
 
     def own_values(u, _):
         dv_sum[u] = own_sum(u)
         return 0
 
     lax.fori_loop(0, OWN, own_values, 0)
-    beside_arrived(1, v_side, v_all)
-    each(0, OWN, output)
-    each(0, 1, backward)
+    each(0, 2, backward, 2)
     finish(0, v_got, lambda u: dv_sum[u], dv_done)
     each(0, OWN, lambda t: send(3, dv_done, dv_out, t))
-    each(1, TILES_DEV, backward)
+    each(2, TILES_DEV, backward, 2)
     send_back(1, 0, k_got, SCALE)
-    each(TILES_DEV, OWN, backward)
+    each(TILES_DEV, OWN, backward, 2)
     send_back(1, 1, k_got, SCALE)
-    each(0, OWN, query_grad)
+    each(0, OWN, query_grad, 2)
     finish(1, k_got, lambda u: own_sum(u) * SCALE, dk_done)
     each(0, OWN, lambda t: send(2, dk_done, dk_out, t))
 

time: 100 us -> 94.1 us (0.941)
  Pallas kernels: 98.3 us -> 93.1 us
    pallas_call x1, Pallas kernels: 95.5 us -> 90.4 us  [body(): pl.pallas_call(kernel, out_shape=results, in_specs=[hbm] * 5, out_specs=(...]
where the time goes in v4:
time: 94.1 us; the launch traced here: 93.9 us
  Pallas kernels  93.1 us (99%)
    pallas_call x1, Pallas kernels, body(): pl.pallas_call(kernel, out_shape=results, in_specs=[hbm] * 5, out_specs=(...  90.4 us
    pallas_call x1, Pallas kernels, body(): pl.pallas_call(hand_over, out_shape=results, in_specs=[hbm] * 4, out_spec...  2.79 us

profile of v4, /device:TPU:1, one launch (start us, length us, event | category | flops | bytes accessed | tf_op | source)
XLA Modules:
  0.0 93.9 jit_solution(7459986672075408249)
XLA Ops:
  0.6 90.4 %shard_map.84 = (bf16[192,2048]{1,0:T(8,128)(2,1)}, bf16[192,2048]{1,0:T(8,128)(2,1)}, bf16[192,2048]{1,0:T(8,128)(2,1)}, bf16[192,2048]{1,0:T(8,128)(2,1)}) custom-call(s32[7,64]{1,0:T(8,128)} %bitcast.1, bf16[192,2048]{1,0:T(8,128)(2,1)} %q_in.1, bf16[192,2048]{1,0:T(8,128)(2,1)} %k_in.1, bf16[192,2048]{1,0:T(8,128)(2,1)} %v_in.1, bf16[192,2048]{1,0:T(8,128)(2,1)} %g_in.1), custom_call_target="tpu_custom_call" | custom-call | tf_op jit(solution)/shard_map/pallas_call | solution.py:441
  91.0 2.8 %shard_map.85 = (bf16[192,2048]{1,0:T(8,128)(2,1)}, bf16[192,2048]{1,0:T(8,128)(2,1)}, bf16[192,2048]{1,0:T(8,128)(2,1)}, bf16[192,2048]{1,0:T(8,128)(2,1)}) custom-call(bf16[192,2048]{1,0:T(8,128)(2,1)} %get-tuple-element.8.refs_0_, bf16[192,2048]{1,0:T(8,128)(2,1)} %get-tuple-element.9.refs_1_, bf16[192,2048]{1,0:T(8,128)(2,1)} %get-tuple-element.10.refs_2_, ...), custom_call_target="tpu_custom_call" | custom-call | tf_op jit(solution)/shard_map/pallas_call | solution.py:463

commit v5 on v4

--- a/solution.py
+++ b/solution.py
@@ -44,6 +44,10 @@
     return there, device(z, y, x_hi, x_lo, 1 - core), near, far, toward
 
 
+def turns(step, core):
+    return jnp.where(step == 0, 2, jnp.where(step == 3, 0, jnp.where((step == 1) == (core == 0), 1, 3)))
+
+
 def head_devices():
     z, y, x_hi, x_lo, core = place()
     found = []
@@ -170,10 +174,10 @@
 
 def kernel(
     rows_in, q_in, k_in, v_in, g_in, o_out, dq_out, dk_out, dv_out,
-    q_own, k_own, v_own, g_own, k_side, v_side, picked, k_all, v_all, score, expo, inv_of, delta_of, terms,
+    q_own, k_own, v_own, g_own, g_0, g_1, g_2, g_3, k_side, v_side, picked, k_all, v_all, score, expo, inv_of, delta_of, terms,
     dv_sum, o_done, dq_done, dk_done, dv_done, part, k_got, v_got,
     rows, slot_of, count_of, own_from, side_from,
-    rows_sem, in_send, in_recv, out_send, out_recv, side_send, side_recv, back_send, back_recv,
+    rows_sem, in_send, in_recv, part_recv, out_send, out_recv, side_send, side_recv, back_send, back_recv,
 ):
     z, y, x_hi, x_lo, core = place()
     is_self = x_lo == core
@@ -185,21 +189,23 @@
     arrays = ((k_in, k_own), (q_in, q_own), (v_in, v_own), (g_in, g_own))
     tile, row = core * 4 + y, pl.multiple_of(x_hi * HALF, HALF)
     targets = head_devices()
+    g_parts = (g_0, g_1, g_2, g_3)
 
     for n, (src, dst) in enumerate(arrays):
         for i, (there, head) in enumerate(targets):
             piece = src.at[:, pl.ds(pl.multiple_of(head * HD, HD), HD)]
-            landing = dst.at[tile, pl.ds(row, HALF)]
+            landing = g_parts[i // 4].at[core, pl.ds(row, HALF)] if n == 3 else dst.at[tile, pl.ds(row, HALF)]
+            sem = part_recv.at[i // 4] if n == 3 else in_recv.at[n]
             if i == 0:
                 @pl.when(is_self)
                 def _():
-                    pltpu.make_async_copy(piece, landing, in_recv.at[n]).start()
+                    pltpu.make_async_copy(piece, landing, sem).start()
 
                 @pl.when(jnp.logical_not(is_self))
                 def _():
-                    pltpu.make_async_remote_copy(piece, landing, in_send.at[n], in_recv.at[n], there, MESH).start()
+                    pltpu.make_async_remote_copy(piece, landing, in_send.at[n], sem, there, MESH).start()
             else:
-                pltpu.make_async_remote_copy(piece, landing, in_send.at[n], in_recv.at[n], there, MESH).start()
+                pltpu.make_async_remote_copy(piece, landing, in_send.at[n], sem, there, MESH).start()
 
     def arrived(n):
         dst = arrays[n][1]
@@ -240,9 +246,7 @@
             whole[OWN + j] = beside[j]
 
     def tile_at(step):
-        turn = step % TILES_DEV
-        away = jnp.where(turn == 0, 2, jnp.where(turn == 3, 0, jnp.where((turn == 1) == (core == 0), 1, 3)))
-        return ((core + step // TILES_DEV) % 2) * TILES_DEV + (y + away) % TILES_DEV
+        return ((core + step // TILES_DEV) % 2) * TILES_DEV + (y + turns(step % TILES_DEV, core)) % TILES_DEV
 
     head = y * 4 + 2 * x_hi + x_lo
 
@@ -293,8 +297,8 @@
     def row(t):
         return expo[pl.ds(t * MAXK, MAXK)].reshape(MAXK * TILE, TILE)
 
-    def value_terms(t):
-        g_scaled = (g_own[t].T.astype(jnp.float32) * inv_of[t]).astype(jnp.bfloat16)
+    def value_terms(t, g):
+        g_scaled = (g.T.astype(jnp.float32) * inv_of[t]).astype(jnp.bfloat16)
         terms[pl.ds(t * MAXK, MAXK)] = dot(row(t), g_scaled, 1, 1).reshape(MAXK, TILE, HD)
 
     def output(t):
@@ -368,10 +372,14 @@
     arrived(2)
     to_sides(1, v_own, v_side, v_all)
     each(5, OWN, weigh)
-    arrived(3)
-    each(0, TILES_DEV, value_terms, 4)
+
+    for away, landed in enumerate(g_parts):
+        pltpu.make_async_copy(landed, landed, part_recv.at[away]).wait()
+        for half in range(2):
+            t = half * TILES_DEV + (y + TILES_DEV - away) % TILES_DEV
+            g_own[t] = landed[half]
+            value_terms(t, landed[half])
     send_back(0, 0, v_got, 1.0)
-    each(TILES_DEV, OWN, value_terms, 4)
     send_back(0, 1, v_got, 1.0)
     beside_arrived(1, v_side, v_all)
     each(0, OWN, output, 2)
@@ -445,6 +453,7 @@
         out_specs=(hbm,) * 4,
         scratch_shapes=[
             tiles(OWN), tiles(OWN), tiles(OWN), tiles(OWN),
+            tiles(2), tiles(2), tiles(2), tiles(2),
             tiles(2 * SIDE), tiles(2 * SIDE), tiles(2, 2 * SIDE), tiles(SLOTS), tiles(SLOTS),
             pltpu.VMEM((MAXK, TILE, TILE), f32),
             pltpu.VMEM((OWN * MAXK, TILE, TILE), jnp.bfloat16),
@@ -455,7 +464,7 @@
             tiles(OWN), tiles(OWN), tiles(OWN), tiles(OWN),
             tiles(2, 2 * SIDE), tiles(2 * SIDE + 1), tiles(2 * SIDE + 1),
             counts(MAXK, 4 * GROUPS), counts(OWN, MAXK), counts(OWN), counts(OWN, OWN), counts(2 * SIDE, TILES_DEV),
-            pltpu.SemaphoreType.DMA, dma((4,)), dma((4,)), dma((4,)), dma((4,)),
+            pltpu.SemaphoreType.DMA, dma((4,)), dma((3,)), dma((4,)), dma((4,)), dma((4,)),
             dma((2, 2)), dma((2, 2)), dma((2, 2, 2)), dma((2, 2, 2)),
         ],
         compiler_params=pltpu.CompilerParams(collective_id=0, has_side_effects=True, vmem_limit_bytes=VMEM_LIMIT),

time: 94.1 us -> 90.8 us (0.965)
  Pallas kernels: 93.1 us -> 89.9 us
    pallas_call x1, Pallas kernels: 90.4 us -> 87.1 us  [body(): pl.pallas_call(kernel, out_shape=results, in_specs=[hbm] * 5, out_specs=(...]
where the time goes in v5:
time: 90.8 us; the launch traced here: 90.7 us
  Pallas kernels  89.9 us (99%)
    pallas_call x1, Pallas kernels, body(): pl.pallas_call(kernel, out_shape=results, in_specs=[hbm] * 5, out_specs=(...  87.1 us
    pallas_call x1, Pallas kernels, body(): pl.pallas_call(hand_over, out_shape=results, in_specs=[hbm] * 4, out_spec...  2.79 us

profile of v5, /device:TPU:1, one launch (start us, length us, event | category | flops | bytes accessed | tf_op | source)
XLA Modules:
  0.0 90.7 jit_solution(14183247045520343519)
XLA Ops:
  0.6 87.1 %shard_map.84 = (bf16[192,2048]{1,0:T(8,128)(2,1)}, bf16[192,2048]{1,0:T(8,128)(2,1)}, bf16[192,2048]{1,0:T(8,128)(2,1)}, bf16[192,2048]{1,0:T(8,128)(2,1)}) custom-call(s32[7,64]{1,0:T(8,128)} %bitcast.1, bf16[192,2048]{1,0:T(8,128)(2,1)} %q_in.1, bf16[192,2048]{1,0:T(8,128)(2,1)} %k_in.1, bf16[192,2048]{1,0:T(8,128)(2,1)} %v_in.1, bf16[192,2048]{1,0:T(8,128)(2,1)} %g_in.1), custom_call_target="tpu_custom_call" | custom-call | tf_op jit(solution)/shard_map/pallas_call | solution.py:449
  87.8 2.8 %shard_map.85 = (bf16[192,2048]{1,0:T(8,128)(2,1)}, bf16[192,2048]{1,0:T(8,128)(2,1)}, bf16[192,2048]{1,0:T(8,128)(2,1)}, bf16[192,2048]{1,0:T(8,128)(2,1)}) custom-call(bf16[192,2048]{1,0:T(8,128)(2,1)} %get-tuple-element.8.refs_0_, bf16[192,2048]{1,0:T(8,128)(2,1)} %get-tuple-element.9.refs_1_, bf16[192,2048]{1,0:T(8,128)(2,1)} %get-tuple-element.10.refs_2_, ...), custom_call_target="tpu_custom_call" | custom-call | tf_op jit(solution)/shard_map/pallas_call | solution.py:472

commit v6 on v5

--- a/solution.py
+++ b/solution.py
@@ -175,7 +175,7 @@
 def kernel(
     rows_in, q_in, k_in, v_in, g_in, o_out, dq_out, dk_out, dv_out,
     q_own, k_own, v_own, g_own, g_0, g_1, g_2, g_3, k_side, v_side, picked, k_all, v_all, score, expo, inv_of, delta_of, terms,
-    dv_sum, o_done, dq_done, dk_done, dv_done, part, k_got, v_got,
+    own_part, o_done, dq_done, dk_done, dv_done, part, k_got, v_got,
     rows, slot_of, count_of, own_from, side_from,
     rows_sem, in_send, in_recv, part_recv, out_send, out_recv, side_send, side_recv, back_send, back_recv,
 ):
@@ -308,6 +308,7 @@
         out = (out * inv_of[t]).astype(jnp.bfloat16)
         o_done[t] = out.T
         send(0, o_done, o_out, t)
+        own_part[t] = own_sum(t)
         delta_of[t] = jnp.sum(g_own[t].T.astype(jnp.float32) * out.astype(jnp.float32), axis=0, keepdims=True)
 
     def backward(t):
@@ -325,6 +326,7 @@
             dq = dq + dot(k_all[slot_of[t, m]], expo[t * MAXK + m], 0, 0)
         dq_done[t] = (dq * (inv_of[t] * SCALE)).astype(jnp.bfloat16).T
         send(1, dq_done, dq_out, t)
+        own_part[t] = own_sum(t) * SCALE
 
     back_copies = {}
 
@@ -351,18 +353,20 @@
             value = value + terms[own_from[u, t]]
         return value
 
-    def finish(n, got, own, done):
+    def finish(n, got, done, sent, out):
         for half in range(2):
             for side in range(2):
                 back_copies[n, half, side].wait_recv()
-        for of_near_tile, start in ((True, near_tile), (False, far_tile)):
-            for inner in range(TILES_DEV):
-                value = own(start + inner)
-                for of_near, slot, low, high in asks:
-                    if of_near == of_near_tile:
-                        at = jnp.where(low == inner, slot, jnp.where(high == inner, slot + 1, 2 * SIDE))
-                        value = value + got[at].astype(jnp.float32)
-                done[start + inner] = value.astype(jnp.bfloat16)
+        for step in range(OWN):
+            t = tile_at(step)
+            inner = t % TILES_DEV
+            value = own_part[t]
+            for of_near, slot, low, high in asks:
+                if of_near == (step < TILES_DEV):
+                    at = jnp.where(low == inner, slot, jnp.where(high == inner, slot + 1, 2 * SIDE))
+                    value = value + got[at].astype(jnp.float32)
+            done[t] = value.astype(jnp.bfloat16)
+            send(sent, done, out, t)
 
     arrived(0)
     to_sides(0, k_own, k_side, k_all)
@@ -384,21 +388,14 @@
     beside_arrived(1, v_side, v_all)
     each(0, OWN, output, 2)
 
-    def own_values(u, _):
-        dv_sum[u] = own_sum(u)
-        return 0
-
-    lax.fori_loop(0, OWN, own_values, 0)
     each(0, 2, backward, 2)
-    finish(0, v_got, lambda u: dv_sum[u], dv_done)
-    each(0, OWN, lambda t: send(3, dv_done, dv_out, t))
+    finish(0, v_got, dv_done, 3, dv_out)
     each(2, TILES_DEV, backward, 2)
     send_back(1, 0, k_got, SCALE)
     each(TILES_DEV, OWN, backward, 2)
     send_back(1, 1, k_got, SCALE)
     each(0, OWN, query_grad, 2)
-    finish(1, k_got, lambda u: own_sum(u) * SCALE, dk_done)
-    each(0, OWN, lambda t: send(2, dk_done, dk_out, t))
+    finish(1, k_got, dk_done, 2, dk_out)
 
     for copy in side_copies + list(back_copies.values()):
         copy.wait_send()

time: 90.8 us -> 90.9 us (level)
  no operation moved by 1% of the time
where the time goes in v6:
time: 90.9 us; the launch traced here: 90.8 us
  Pallas kernels  90 us (99%)
    pallas_call x1, Pallas kernels, body(): pl.pallas_call(kernel, out_shape=results, in_specs=[hbm] * 5, out_specs=(...  87.2 us
    pallas_call x1, Pallas kernels, body(): pl.pallas_call(hand_over, out_shape=results, in_specs=[hbm] * 4, out_spec...  2.79 us

profile of v6, /device:TPU:1, one launch (start us, length us, event | category | flops | bytes accessed | tf_op | source)
XLA Modules:
  0.0 90.8 jit_solution(17037368933663606278)
XLA Ops:
  0.6 87.2 %shard_map.84 = (bf16[192,2048]{1,0:T(8,128)(2,1)}, bf16[192,2048]{1,0:T(8,128)(2,1)}, bf16[192,2048]{1,0:T(8,128)(2,1)}, bf16[192,2048]{1,0:T(8,128)(2,1)}) custom-call(s32[7,64]{1,0:T(8,128)} %bitcast.1, bf16[192,2048]{1,0:T(8,128)(2,1)} %q_in.1, bf16[192,2048]{1,0:T(8,128)(2,1)} %k_in.1, bf16[192,2048]{1,0:T(8,128)(2,1)} %v_in.1, bf16[192,2048]{1,0:T(8,128)(2,1)} %g_in.1), custom_call_target="tpu_custom_call" | custom-call | tf_op jit(solution)/shard_map/pallas_call | solution.py:446
  87.8 2.8 %shard_map.85 = (bf16[192,2048]{1,0:T(8,128)(2,1)}, bf16[192,2048]{1,0:T(8,128)(2,1)}, bf16[192,2048]{1,0:T(8,128)(2,1)}, bf16[192,2048]{1,0:T(8,128)(2,1)}) custom-call(bf16[192,2048]{1,0:T(8,128)(2,1)} %get-tuple-element.8.refs_0_, bf16[192,2048]{1,0:T(8,128)(2,1)} %get-tuple-element.9.refs_1_, bf16[192,2048]{1,0:T(8,128)(2,1)} %get-tuple-element.10.refs_2_, ...), custom_call_target="tpu_custom_call" | custom-call | tf_op jit(solution)/shard_map/pallas_call | solution.py:469

commit v7 on v6

--- a/solution.py
+++ b/solution.py
@@ -326,7 +326,6 @@
             dq = dq + dot(k_all[slot_of[t, m]], expo[t * MAXK + m], 0, 0)
         dq_done[t] = (dq * (inv_of[t] * SCALE)).astype(jnp.bfloat16).T
         send(1, dq_done, dq_out, t)
-        own_part[t] = own_sum(t) * SCALE
 
     back_copies = {}
 
@@ -392,9 +391,16 @@
     finish(0, v_got, dv_done, 3, dv_out)
     each(2, TILES_DEV, backward, 2)
     send_back(1, 0, k_got, SCALE)
+    each(0, TILES_DEV, query_grad, 2)
     each(TILES_DEV, OWN, backward, 2)
     send_back(1, 1, k_got, SCALE)
-    each(0, OWN, query_grad, 2)
+    each(TILES_DEV, OWN, query_grad, 2)
+
+    def own_keys(u, _):
+        own_part[u] = own_sum(u) * SCALE
+        return 0
+
+    lax.fori_loop(0, OWN, own_keys, 0)
     finish(1, k_got, dk_done, 2, dk_out)
 
     for copy in side_copies + list(back_copies.values()):

time: 90.9 us -> 90.9 us (level)
  no operation moved by 1% of the time
where the time goes in v7:
time: 90.9 us; the launch traced here: 90.8 us
  Pallas kernels  90 us (99%)
    pallas_call x1, Pallas kernels, body(): pl.pallas_call(kernel, out_shape=results, in_specs=[hbm] * 5, out_specs=(...  87.2 us
    pallas_call x1, Pallas kernels, body(): pl.pallas_call(hand_over, out_shape=results, in_specs=[hbm] * 4, out_spec...  2.79 us

profile of v7, /device:TPU:1, one launch (start us, length us, event | category | flops | bytes accessed | tf_op | source)
XLA Modules:
  0.0 90.8 jit_solution(16549482599210334937)
XLA Ops:
  0.6 87.2 %shard_map.84 = (bf16[192,2048]{1,0:T(8,128)(2,1)}, bf16[192,2048]{1,0:T(8,128)(2,1)}, bf16[192,2048]{1,0:T(8,128)(2,1)}, bf16[192,2048]{1,0:T(8,128)(2,1)}) custom-call(s32[7,64]{1,0:T(8,128)} %bitcast.1, bf16[192,2048]{1,0:T(8,128)(2,1)} %q_in.1, bf16[192,2048]{1,0:T(8,128)(2,1)} %k_in.1, bf16[192,2048]{1,0:T(8,128)(2,1)} %v_in.1, bf16[192,2048]{1,0:T(8,128)(2,1)} %g_in.1), custom_call_target="tpu_custom_call" | custom-call | tf_op jit(solution)/shard_map/pallas_call | solution.py:452
  87.9 2.8 %shard_map.85 = (bf16[192,2048]{1,0:T(8,128)(2,1)}, bf16[192,2048]{1,0:T(8,128)(2,1)}, bf16[192,2048]{1,0:T(8,128)(2,1)}, bf16[192,2048]{1,0:T(8,128)(2,1)}) custom-call(bf16[192,2048]{1,0:T(8,128)(2,1)} %get-tuple-element.8.refs_0_, bf16[192,2048]{1,0:T(8,128)(2,1)} %get-tuple-element.9.refs_1_, bf16[192,2048]{1,0:T(8,128)(2,1)} %get-tuple-element.10.refs_2_, ...), custom_call_target="tpu_custom_call" | custom-call | tf_op jit(solution)/shard_map/pallas_call | solution.py:475
